TPU v7x, 256 devices: a whole 4x4x8 slice. The times are simulated.
256 devices in a mesh: gx: 16 (over y, z_hi), gy: 16 (over z_lo, x, core).
Axes of the slice: x: 4, y: 4, z: 8 (z_hi: 4, z_lo: 2; z = z_hi * 2 + z_lo), core: 2. Of those that a mesh axis runs over, the one named last changes fastest.
Arguments:
- ensemble: float32 [80, 4, 128, 2048], P(None, None, 'gx', 'gy'), may hold values from -6 to 6
- obs_x: int32 [2, 1024], replicated, may hold values from 0 to 7
- obs_y: int32 [2, 1024], replicated, may hold values from 0 to 127
- obs_level: int32 [2, 1024], replicated, may hold values from 0 to 3
- owner_row: int32 [2], replicated, may hold values from 0 to 15
- owner_col: int32 [2], replicated, may hold values from 0 to 15
- obs_value: float32 [2, 1024], replicated, may hold values from -6 to 6
- obs_noise: float32 [2, 80, 1024], replicated, may hold values from -5 to 5
- obs_var: float32 [2, 1024], replicated, may hold values from 0.25 to 4
Outputs:
- posterior: float32 [80, 4, 128, 2048], P(None, None, 'gx', 'gy')
Inputs may be any that keep to these rules, and one draw needn't show every extreme that they name: `owner_row`: gx index of the tile holding batch b's observations. `owner_col`: gy index of the tile holding batch b's observations.
All inputs are finite; a program needn't handle non-finite values.
Results may differ from a plain program's by a relative error of at most 0.0003.
Values sent between devices are 32-bit elements; how exact they have to be, the bound alone decides.
A program may use at most 128 MiB of HBM per device.

v0:
```python
import jax
import jax.numpy as jnp
from jax import lax
from jax.sharding import PartitionSpec as P

LOC = 64


HIGH = lax.Precision.HIGHEST


def from_behind(x, axis, by):
    size = lax.axis_size(axis)
    pairs = [(i, i + by) for i in range(size) if 0 <= i + by < size]
    return lax.ppermute(x, axis, pairs)


def taper_of(dx, dy, dlev, radius):
    dist = (dx * dx + dy * dy).astype(jnp.float32) / jnp.float32(radius * radius)
    inner = jnp.maximum(jnp.float32(1.0) - dist, jnp.float32(0.0))
    return inner * inner / (jnp.float32(1.0) + jnp.abs(dlev).astype(jnp.float32))


def pick_cells(state, levels, local_x, local_y):
    members, level_count, tile_x, tile_y = state.shape
    count = levels.shape[0]
    select_y = (jnp.arange(tile_y, dtype=jnp.int32)[:, None] == local_y[None, :]).astype(
        jnp.float32
    )
    select_x = (jnp.arange(tile_x, dtype=jnp.int32)[:, None] == local_x[None, :]).astype(
        jnp.float32
    )
    select_l = (jnp.arange(level_count, dtype=jnp.int32)[:, None] == levels[None, :]).astype(
        jnp.float32
    )
    partial_rows = jnp.dot(
        state.reshape(members * level_count * tile_x, tile_y),
        select_y,
        precision=HIGH,
        preferred_element_type=jnp.float32,
    )
    partial_rows = partial_rows.reshape(members, level_count, tile_x, count)
    chooser = select_l[:, None, :] * select_x[None, :, :]
    return jnp.sum(partial_rows * chooser[None], axis=(1, 2))


def gauss_jordan(matrix, rhs):
    order = matrix.shape[0]
    joined = jnp.concatenate([matrix, rhs], axis=1)
    row_ids = jnp.arange(order, dtype=jnp.int32)
    col_ids = jnp.arange(joined.shape[1], dtype=jnp.int32)

    def eliminate(step, current):
        row_pick = (row_ids == step).astype(jnp.float32)
        col_pick = (col_ids == step).astype(jnp.float32)
        pivot_row = jnp.sum(current * row_pick[:, None], axis=0)
        pivot = jnp.sum(pivot_row * col_pick)
        pivot_row = pivot_row / pivot
        column = jnp.sum(current * col_pick[None, :], axis=1)
        reduced = current - column[:, None] * pivot_row[None, :]
        return jnp.where((row_ids == step)[:, None], pivot_row[None, :], reduced)

    joined = lax.fori_loop(0, order, eliminate, joined)
    return joined[:, order:]


def weights_small(obs_anom, innovation, variance, members):
    inv_var = 1.0 / variance
    scaled = obs_anom * inv_var[None, :]
    inner = jnp.dot(scaled, obs_anom.T, precision=HIGH, preferred_element_type=jnp.float32)
    inner = inner + (members - 1) * jnp.eye(members, dtype=jnp.float32)
    project = jnp.dot(scaled, innovation.T, precision=HIGH, preferred_element_type=jnp.float32)
    solved = gauss_jordan(inner, project)
    correction = jnp.dot(solved.T, scaled, precision=HIGH, preferred_element_type=jnp.float32)
    return innovation * inv_var[None, :] - correction


def shards(ensemble, obs_x, obs_y, obs_level, owner_row, owner_col, obs_value, obs_noise, obs_var):
    members, levels_here, tile_x, tile_y = ensemble.shape
    batches = obs_x.shape[0]
    size_x = lax.axis_size("gx")
    size_y = lax.axis_size("gy")
    row_here = lax.axis_index("gx")
    col_here = lax.axis_index("gy")
    reach_x = min((LOC - 2 + tile_x) // tile_x, size_x - 1)
    reach_y = min((LOC - 2 + tile_y) // tile_y, size_y - 1)
    cell_x = row_here * tile_x + jnp.arange(tile_x, dtype=jnp.int32)
    cell_y = col_here * tile_y + jnp.arange(tile_y, dtype=jnp.int32)
    state = ensemble
    for batch in range(batches):
        row = owner_row[batch]
        col = owner_col[batch]
        levels = obs_level[batch]
        local_hx = pick_cells(state, levels, obs_x[batch], obs_y[batch])
        owned = jnp.logical_and(row_here == row, col_here == col)
        piece = jnp.where(owned, local_hx, jnp.float32(0.0))
        across = piece
        for offset in list(range(1, reach_x + 1)) + list(range(-reach_x, 0)):
            across = across + from_behind(piece, "gx", offset)
        prior_hx = across
        for offset in list(range(1, reach_y + 1)) + list(range(-reach_y, 0)):
            prior_hx = prior_hx + from_behind(across, "gy", offset)
        obs_anom = prior_hx - jnp.mean(prior_hx, axis=0)
        innovation = obs_value[batch][None, :] + obs_noise[batch] - prior_hx
        weights = weights_small(obs_anom, innovation, obs_var[batch], members)
        glob_x = row * tile_x + obs_x[batch]
        glob_y = col * tile_y + obs_y[batch]
        anomaly = state - jnp.mean(state, axis=0)
        dx = cell_x[:, None, None] - glob_x[None, None, :]
        dy = cell_y[None, :, None] - glob_y[None, None, :]
        updated = []
        for level in range(levels_here):
            slab = anomaly[:, level].reshape(members, tile_x * tile_y)
            cross = jnp.dot(
                slab.T, obs_anom, precision=HIGH, preferred_element_type=jnp.float32
            ) / (members - 1)
            taper = taper_of(dx, dy, level - levels[None, None, :], LOC).reshape(
                tile_x * tile_y, -1
            )
            change = jnp.dot(
                weights, (taper * cross).T, precision=HIGH, preferred_element_type=jnp.float32
            )
            updated.append(state[:, level] + change.reshape(members, tile_x, tile_y))
        state = jnp.stack(updated, axis=1)
    return state


def solution(mesh):
    in_specs = (P(None, None, "gx", "gy"), P(), P(), P(), P(), P(), P(), P(), P())
    out_specs = P(None, None, "gx", "gy")
    return jax.shard_map(shards, mesh=mesh, in_specs=in_specs, out_specs=out_specs, check_vma=False)
```

profile of v0, /device:TPU:74, one launch (start us, length us, event | category | flops | bytes accessed | tf_op | source)
XLA Modules:
  0.0 663.0 jit_solution(15731712564876416691)
XLA Ops:
  0.8 8.2 %convolution_bitcast_fusion = f32[2560,1024]{0,1:T(8,128)} fusion(f32[2560,128]{1,0:T(8,128)} %bitcast.169, s32[1024]{0:T(1024)S(1)} %bitcast.182), kind=kOutput, calls=%fused_computation.26 | convolution fusion | flops 4026793984 | bytes 11800576 | tf_op jit(solution)/shard_map/dot_general | solution.py:36
  9.0 11.4 %copy.14 = f32[2560,1024]{1,0:T(8,128)} copy(f32[2560,1024]{0,1:T(8,128)} %convolution_bitcast_fusion) | data formatting | bytes 20971520 | tf_op jit(solution)/shard_map/dot_general | solution.py:36
  21.7 6.0 multiply_reduce_fusion.5
  31.7 8.6 %collective-permute-start.14 = (f32[80,1024]{1,0:T(8,128)}, f32[80,1024]{1,0:T(8,128)S(1)}, u32[]{:S(2)}, u32[]{:S(2)}) collective-permute-start(f32[80,1024]{1,0:T(8,128)} %broadcast_select_fusion.1), channel_id=1, source_target_pairs={{32,0},{48,16},{64,32},{80,48},{96,64},{112,80},{128,96},{144,112}... | collective-permute-start | bytes 983048 | tf_op jit(solution)/shard_map/ppermute | solution.py:15
  49.5 8.7 %collective-permute-done.15 = f32[80,1024]{1,0:T(8,128)S(1)} collective-permute-done((f32[80,1024]{1,0:T(8,128)}, f32[80,1024]{1,0:T(8,128)S(1)}, u32[]{:S(2)}, u32[]{:S(2)}) %collective-permute-start.15) | collective-permute-done | bytes 327712 | tf_op jit(solution)/shard_map/ppermute | solution.py:15
  62.0 13.6 %collective-permute-done.13 = f32[80,1024]{1,0:T(8,128)S(1)} collective-permute-done((f32[80,1024]{1,0:T(8,128)}, f32[80,1024]{1,0:T(8,128)S(1)}, u32[]{:S(2)}, u32[]{:S(2)}) %collective-permute-start.13) | collective-permute-done | bytes 327712 | tf_op jit(solution)/shard_map/ppermute | solution.py:15
  76.9 7.5 %collective-permute-start.7 = (f32[80,1024]{1,0:T(8,128)}, f32[80,1024]{1,0:T(8,128)}, u32[]{:S(2)}, u32[]{:S(2)}) collective-permute-start(f32[80,1024]{1,0:T(8,128)} %broadcast_select_fusion.1), channel_id=1, source_target_pairs={{0,128},{16,144},{32,160},{48,176},{64,192},{80,208},{96,224},{112... | collective-permute-start | bytes 983048 | tf_op jit(solution)/shard_map/ppermute | solution.py:15
  86.4 6.9 %collective-permute-start.5 = (f32[80,1024]{1,0:T(8,128)}, f32[80,1024]{1,0:T(8,128)}, u32[]{:S(2)}, u32[]{:S(2)}) collective-permute-start(f32[80,1024]{1,0:T(8,128)} %broadcast_select_fusion.1), channel_id=1, source_target_pairs={{0,96},{16,112},{32,128},{48,144},{64,160},{80,176},{96,192},{112,... | collective-permute-start | bytes 983048 | tf_op jit(solution)/shard_map/ppermute | solution.py:15
  102.9 5.9 collective-permute-start.2
  108.8 13.6 %collective-permute-start.1 = (f32[80,1024]{1,0:T(8,128)}, f32[80,1024]{1,0:T(8,128)}, u32[]{:S(2)}, u32[]{:S(2)}) collective-permute-start(f32[80,1024]{1,0:T(8,128)} %broadcast_select_fusion.1), channel_id=1, source_target_pairs={{0,32},{16,48},{32,64},{48,80},{64,96},{80,112},{96,128},{112,144}... | collective-permute-start | bytes 983048 | tf_op jit(solution)/shard_map/ppermute | solution.py:15
  122.4 14.7 %collective-permute-start = (f32[80,1024]{1,0:T(8,128)}, f32[80,1024]{1,0:T(8,128)}, u32[]{:S(2)}, u32[]{:S(2)}) collective-permute-start(f32[80,1024]{1,0:T(8,128)} %broadcast_select_fusion.1), channel_id=1, source_target_pairs={{0,16},{16,32},{32,48},{48,64},{64,80},{80,96},{96,112},{112,128},... | collective-permute-start | bytes 983048 | tf_op jit(solution)/shard_map/ppermute | solution.py:15
  140.3 20.5 %collective-permute-done.1 = f32[80,1024]{1,0:T(8,128)} collective-permute-done((f32[80,1024]{1,0:T(8,128)}, f32[80,1024]{1,0:T(8,128)}, u32[]{:S(2)}, u32[]{:S(2)}) %collective-permute-start.1) | collective-permute-done | bytes 327712 | tf_op jit(solution)/shard_map/ppermute | solution.py:15
  165.7 13.9 %collective-permute-start.16 = (f32[80,1024]{1,0:T(8,128)S(1)}, f32[80,1024]{1,0:T(8,128)S(1)}, u32[]{:S(2)}, u32[]{:S(2)}) collective-permute-start(f32[80,1024]{1,0:T(8,128)S(1)} %add_add_fusion.3), channel_id=1, source_target_pairs={{0,1},{1,2},{2,3},{3,4},{4,5},{5,6},{6,7},{7,8},{8,9},{9,10},{10,1... | collective-permute-start | bytes 983048 | tf_op jit(solution)/shard_map/ppermute | solution.py:15
  183.5 126.7 %while.28 = (s32[]{:T(128)}, f32[80,160]{1,0:T(8,128)S(1)}, s32[]{:T(128)}) while((s32[]{:T(128)}, f32[80,160]{1,0:T(8,128)S(1)}, s32[]{:T(128)}) %tuple.95), condition=%wide.region_6.7_spmd.clone, body=%wide.region_2.6_spmd.clone.sunk | while | flops 90481 | bytes 159593 | solution.py:63
  310.7 7.2 %fusion.20 = f32[1024,1024]{1,0:T(8,128)S(1)} fusion(f32[8,128,1024]{2,1,0:T(8,128)} %maximum_multiply_fusion.1, f32[1024]{0:T(1024)S(1)} %copy-done.24, f32[10,8,8,128]{3,2,1,0:T(8,128)S(1)} %bitcast.177, f32[80,1024]{1,0:T(8,128)S(1)} %get-tuple-element.194, f32[1024]{0:T(1024)S(1)} %broadcast_multiply_fusion.5), kind=kOutput, calls=%fused_computation.39 | convolution fusion | flops 1009860608 | bytes 9052160 | tf_op jit(solution)/shard_map/dot_general | solution.py:114
  317.9 4.2 convolution_bitcast_fusion.8
  326.1 4.2 convolution_bitcast_fusion.7
  330.4 4.3 fusion.23
  347.6 5.1 multiply_reduce_fusion.4
  352.7 8.5 %collective-permute-start.33 = (f32[80,1024]{1,0:T(8,128)S(1)}, f32[80,1024]{1,0:T(8,128)S(1)}, u32[]{:S(2)}, u32[]{:S(2)}) collective-permute-start(f32[80,1024]{1,0:T(8,128)S(1)} %broadcast_select_fusion), channel_id=1, source_target_pairs={{16,0},{32,16},{48,32},{64,48},{80,64},{96,80},{112,96},{128,112},... | collective-permute-start | bytes 983048 | tf_op jit(solution)/shard_map/ppermute | solution.py:15
  368.9 29.4 %collective-permute-done.33 = f32[80,1024]{1,0:T(8,128)S(1)} collective-permute-done((f32[80,1024]{1,0:T(8,128)S(1)}, f32[80,1024]{1,0:T(8,128)S(1)}, u32[]{:S(2)}, u32[]{:S(2)}) %collective-permute-start.33) | collective-permute-done | bytes 327712 | tf_op jit(solution)/shard_map/ppermute | solution.py:15
  402.2 6.1 collective-permute-start.25
  412.3 8.5 %collective-permute-done.28 = f32[80,1024]{1,0:T(8,128)S(1)} collective-permute-done((f32[80,1024]{1,0:T(8,128)S(1)}, f32[80,1024]{1,0:T(8,128)S(1)}, u32[]{:S(2)}, u32[]{:S(2)}) %collective-permute-start.28) | collective-permute-done | bytes 327712 | tf_op jit(solution)/shard_map/ppermute | solution.py:15
  424.9 15.0 %collective-permute-start.22 = (f32[80,1024]{1,0:T(8,128)S(1)}, f32[80,1024]{1,0:T(8,128)S(1)}, u32[]{:S(2)}, u32[]{:S(2)}) collective-permute-start(f32[80,1024]{1,0:T(8,128)S(1)} %broadcast_select_fusion), channel_id=1, source_target_pairs={{0,80},{16,96},{32,112},{48,128},{64,144},{80,160},{96,176},{112,1... | collective-permute-start | bytes 983048 | tf_op jit(solution)/shard_map/ppermute | solution.py:15
  443.8 4.3 collective-permute-start.19
  448.0 10.4 %collective-permute-start.18 = (f32[80,1024]{1,0:T(8,128)S(1)}, f32[80,1024]{1,0:T(8,128)S(1)}, u32[]{:S(2)}, u32[]{:S(2)}) collective-permute-start(f32[80,1024]{1,0:T(8,128)S(1)} %broadcast_select_fusion), channel_id=1, source_target_pairs={{0,16},{16,32},{32,48},{48,64},{64,80},{80,96},{96,112},{112,128},... | collective-permute-start | bytes 983048 | tf_op jit(solution)/shard_map/ppermute | solution.py:15
  459.2 10.1 %collective-permute-done.21 = f32[80,1024]{1,0:T(8,128)S(1)} collective-permute-done((f32[80,1024]{1,0:T(8,128)S(1)}, f32[80,1024]{1,0:T(8,128)S(1)}, u32[]{:S(2)}, u32[]{:S(2)}) %collective-permute-start.21) | collective-permute-done | bytes 327712 | tf_op jit(solution)/shard_map/ppermute | solution.py:15
  473.3 17.8 %collective-permute-done.18 = f32[80,1024]{1,0:T(8,128)S(1)} collective-permute-done((f32[80,1024]{1,0:T(8,128)S(1)}, f32[80,1024]{1,0:T(8,128)S(1)}, u32[]{:S(2)}, u32[]{:S(2)}) %collective-permute-start.18) | collective-permute-done | bytes 327712 | tf_op jit(solution)/shard_map/ppermute | solution.py:15
  503.0 121.2 %while.29 = (s32[]{:T(128)}, f32[80,160]{1,0:T(8,128)S(1)}, s32[]{:T(128)}) while((s32[]{:T(128)}, f32[80,160]{1,0:T(8,128)S(1)}, s32[]{:T(128)}) %tuple.98), condition=%wide.region_14.15_spmd.clone, body=%wide.region_10.14_spmd.clone.sunk | while | flops 90481 | bytes 159593 | solution.py:63
  624.8 7.4 %fusion.19 = f32[1024,1024]{1,0:T(8,128)S(1)} fusion(f32[8,128,1024]{2,1,0:T(8,128)} %maximum_multiply_fusion, f32[1024]{0:T(1024)S(1)} %get-tuple-element.222, f32[10,8,8,128]{3,2,1,0:T(8,128)S(1)} %bitcast.181, f32[80,1024]{1,0:T(8,128)S(1)} %get-tuple-element.192, f32[1024]{0:T(1024)S(1)} %broadcast_multiply_fusion.4), kind=kOutput, calls=%fused_computation.34 | convolution fusion | flops 1009860608 | bytes 9052160 | tf_op jit(solution)/shard_map/dot_general | solution.py:114
  640.4 4.2 convolution_bitcast_fusion.2
  644.7 4.2 fusion.17
  (1139 shorter events, 359.2 us)
Async XLA Ops:
  29.8 28.5 %collective-permute-start.15 = (f32[80,1024]{1,0:T(8,128)}, f32[80,1024]{1,0:T(8,128)S(1)}, u32[]{:S(2)}, u32[]{:S(2)}) collective-permute-start(f32[80,1024]{1,0:T(8,128)} %broadcast_select_fusion.1), channel_id=1, source_target_pairs={{16,0},{32,16},{48,32},{64,48},{80,64},{96,80},{112,96},{128,112},... | collective-permute-start | bytes 983048 | tf_op jit(solution)/shard_map/ppermute | solution.py:15
  31.7 29.0 %collective-permute-start.14 = (f32[80,1024]{1,0:T(8,128)}, f32[80,1024]{1,0:T(8,128)S(1)}, u32[]{:S(2)}, u32[]{:S(2)}) collective-permute-start(f32[80,1024]{1,0:T(8,128)} %broadcast_select_fusion.1), channel_id=1, source_target_pairs={{32,0},{48,16},{64,32},{80,48},{96,64},{112,80},{128,96},{144,112}... | collective-permute-start | bytes 983048 | tf_op jit(solution)/shard_map/ppermute | solution.py:15
  40.3 35.3 %collective-permute-start.13 = (f32[80,1024]{1,0:T(8,128)}, f32[80,1024]{1,0:T(8,128)S(1)}, u32[]{:S(2)}, u32[]{:S(2)}) collective-permute-start(f32[80,1024]{1,0:T(8,128)} %broadcast_select_fusion.1), channel_id=1, source_target_pairs={{48,0},{64,16},{80,32},{96,48},{112,64},{128,80},{144,96},{160,112... | collective-permute-start | bytes 983048 | tf_op jit(solution)/shard_map/ppermute | solution.py:15
  42.3 34.6 %collective-permute-start.12 = (f32[80,1024]{1,0:T(8,128)}, f32[80,1024]{1,0:T(8,128)S(1)}, u32[]{:S(2)}, u32[]{:S(2)}) collective-permute-start(f32[80,1024]{1,0:T(8,128)} %broadcast_select_fusion.1), channel_id=1, source_target_pairs={{64,0},{80,16},{96,32},{112,48},{128,64},{144,80},{160,96},{176,11... | collective-permute-start | bytes 983048 | tf_op jit(solution)/shard_map/ppermute | solution.py:15
  44.2 40.2 %collective-permute-start.11 = (f32[80,1024]{1,0:T(8,128)}, f32[80,1024]{1,0:T(8,128)S(1)}, u32[]{:S(2)}, u32[]{:S(2)}) collective-permute-start(f32[80,1024]{1,0:T(8,128)} %broadcast_select_fusion.1), channel_id=1, source_target_pairs={{80,0},{96,16},{112,32},{128,48},{144,64},{160,80},{176,96},{192,1... | collective-permute-start | bytes 983048 | tf_op jit(solution)/shard_map/ppermute | solution.py:15
  58.2 28.1 %collective-permute-start.10 = (f32[80,1024]{1,0:T(8,128)}, f32[80,1024]{1,0:T(8,128)S(1)}, u32[]{:S(2)}, u32[]{:S(2)}) collective-permute-start(f32[80,1024]{1,0:T(8,128)} %broadcast_select_fusion.1), channel_id=1, source_target_pairs={{96,0},{112,16},{128,32},{144,48},{160,64},{176,80},{192,96},{208,... | collective-permute-start | bytes 983048 | tf_op jit(solution)/shard_map/ppermute | solution.py:15
  60.7 36.9 %collective-permute-start.9 = (f32[80,1024]{1,0:T(8,128)}, f32[80,1024]{1,0:T(8,128)}, u32[]{:S(2)}, u32[]{:S(2)}) collective-permute-start(f32[80,1024]{1,0:T(8,128)} %broadcast_select_fusion.1), channel_id=1, source_target_pairs={{112,0},{128,16},{144,32},{160,48},{176,64},{192,80},{208,96},{224... | collective-permute-start | bytes 983048 | tf_op jit(solution)/shard_map/ppermute | solution.py:15
  75.6 23.9 %collective-permute-start.8 = (f32[80,1024]{1,0:T(8,128)}, f32[80,1024]{1,0:T(8,128)}, u32[]{:S(2)}, u32[]{:S(2)}) collective-permute-start(f32[80,1024]{1,0:T(8,128)} %broadcast_select_fusion.1), channel_id=1, source_target_pairs={{128,0},{144,16},{160,32},{176,48},{192,64},{208,80},{224,96},{240... | collective-permute-start | bytes 983048 | tf_op jit(solution)/shard_map/ppermute | solution.py:15
  76.9 26.0 %collective-permute-start.7 = (f32[80,1024]{1,0:T(8,128)}, f32[80,1024]{1,0:T(8,128)}, u32[]{:S(2)}, u32[]{:S(2)}) collective-permute-start(f32[80,1024]{1,0:T(8,128)} %broadcast_select_fusion.1), channel_id=1, source_target_pairs={{0,128},{16,144},{32,160},{48,176},{64,192},{80,208},{96,224},{112... | collective-permute-start | bytes 983048 | tf_op jit(solution)/shard_map/ppermute | solution.py:15
  84.4 24.4 %collective-permute-start.6 = (f32[80,1024]{1,0:T(8,128)}, f32[80,1024]{1,0:T(8,128)}, u32[]{:S(2)}, u32[]{:S(2)}) collective-permute-start(f32[80,1024]{1,0:T(8,128)} %broadcast_select_fusion.1), channel_id=1, source_target_pairs={{0,112},{16,128},{32,144},{48,160},{64,176},{80,192},{96,208},{112... | collective-permute-start | bytes 983048 | tf_op jit(solution)/shard_map/ppermute | solution.py:15
  86.4 36.0 %collective-permute-start.5 = (f32[80,1024]{1,0:T(8,128)}, f32[80,1024]{1,0:T(8,128)}, u32[]{:S(2)}, u32[]{:S(2)}) collective-permute-start(f32[80,1024]{1,0:T(8,128)} %broadcast_select_fusion.1), channel_id=1, source_target_pairs={{0,96},{16,112},{32,128},{48,144},{64,160},{80,176},{96,192},{112,... | collective-permute-start | bytes 983048 | tf_op jit(solution)/shard_map/ppermute | solution.py:15
  97.6 42.7 %collective-permute-start.4 = (f32[80,1024]{1,0:T(8,128)}, f32[80,1024]{1,0:T(8,128)}, u32[]{:S(2)}, u32[]{:S(2)}) collective-permute-start(f32[80,1024]{1,0:T(8,128)} %broadcast_select_fusion.1), channel_id=1, source_target_pairs={{0,80},{16,96},{32,112},{48,128},{64,144},{80,160},{96,176},{112,1... | collective-permute-start | bytes 983048 | tf_op jit(solution)/shard_map/ppermute | solution.py:15
  99.5 40.8 %collective-permute-start.3 = (f32[80,1024]{1,0:T(8,128)}, f32[80,1024]{1,0:T(8,128)}, u32[]{:S(2)}, u32[]{:S(2)}) collective-permute-start(f32[80,1024]{1,0:T(8,128)} %broadcast_select_fusion.1), channel_id=1, source_target_pairs={{0,64},{16,80},{32,96},{48,112},{64,128},{80,144},{96,160},{112,17... | collective-permute-start | bytes 983048 | tf_op jit(solution)/shard_map/ppermute | solution.py:15
  102.9 37.3 %collective-permute-start.2 = (f32[80,1024]{1,0:T(8,128)}, f32[80,1024]{1,0:T(8,128)}, u32[]{:S(2)}, u32[]{:S(2)}) collective-permute-start(f32[80,1024]{1,0:T(8,128)} %broadcast_select_fusion.1), channel_id=1, source_target_pairs={{0,48},{16,64},{32,80},{48,96},{64,112},{80,128},{96,144},{112,160... | collective-permute-start | bytes 983048 | tf_op jit(solution)/shard_map/ppermute | solution.py:15
  108.8 51.9 %collective-permute-start.1 = (f32[80,1024]{1,0:T(8,128)}, f32[80,1024]{1,0:T(8,128)}, u32[]{:S(2)}, u32[]{:S(2)}) collective-permute-start(f32[80,1024]{1,0:T(8,128)} %broadcast_select_fusion.1), channel_id=1, source_target_pairs={{0,32},{16,48},{32,64},{48,80},{64,96},{80,112},{96,128},{112,144}... | collective-permute-start | bytes 983048 | tf_op jit(solution)/shard_map/ppermute | solution.py:15
  122.4 38.3 %collective-permute-start = (f32[80,1024]{1,0:T(8,128)}, f32[80,1024]{1,0:T(8,128)}, u32[]{:S(2)}, u32[]{:S(2)}) collective-permute-start(f32[80,1024]{1,0:T(8,128)} %broadcast_select_fusion.1), channel_id=1, source_target_pairs={{0,16},{16,32},{32,48},{48,64},{64,80},{80,96},{96,112},{112,128},... | collective-permute-start | bytes 983048 | tf_op jit(solution)/shard_map/ppermute | solution.py:15
  352.7 45.5 %collective-permute-start.33 = (f32[80,1024]{1,0:T(8,128)S(1)}, f32[80,1024]{1,0:T(8,128)S(1)}, u32[]{:S(2)}, u32[]{:S(2)}) collective-permute-start(f32[80,1024]{1,0:T(8,128)S(1)} %broadcast_select_fusion), channel_id=1, source_target_pairs={{16,0},{32,16},{48,32},{64,48},{80,64},{96,80},{112,96},{128,112},... | collective-permute-start | bytes 983048 | tf_op jit(solution)/shard_map/ppermute | solution.py:15
  361.2 38.4 %collective-permute-start.32 = (f32[80,1024]{1,0:T(8,128)S(1)}, f32[80,1024]{1,0:T(8,128)S(1)}, u32[]{:S(2)}, u32[]{:S(2)}) collective-permute-start(f32[80,1024]{1,0:T(8,128)S(1)} %broadcast_select_fusion), channel_id=1, source_target_pairs={{32,0},{48,16},{64,32},{80,48},{96,64},{112,80},{128,96},{144,112}... | collective-permute-start | bytes 983048 | tf_op jit(solution)/shard_map/ppermute | solution.py:15
  363.1 37.7 %collective-permute-start.31 = (f32[80,1024]{1,0:T(8,128)S(1)}, f32[80,1024]{1,0:T(8,128)S(1)}, u32[]{:S(2)}, u32[]{:S(2)}) collective-permute-start(f32[80,1024]{1,0:T(8,128)S(1)} %broadcast_select_fusion), channel_id=1, source_target_pairs={{48,0},{64,16},{80,32},{96,48},{112,64},{128,80},{144,96},{160,112... | collective-permute-start | bytes 983048 | tf_op jit(solution)/shard_map/ppermute | solution.py:15
  365.0 37.1 %collective-permute-start.30 = (f32[80,1024]{1,0:T(8,128)S(1)}, f32[80,1024]{1,0:T(8,128)S(1)}, u32[]{:S(2)}, u32[]{:S(2)}) collective-permute-start(f32[80,1024]{1,0:T(8,128)S(1)} %broadcast_select_fusion), channel_id=1, source_target_pairs={{64,0},{80,16},{96,32},{112,48},{128,64},{144,80},{160,96},{176,11... | collective-permute-start | bytes 983048 | tf_op jit(solution)/shard_map/ppermute | solution.py:15
  367.0 44.0 %collective-permute-start.29 = (f32[80,1024]{1,0:T(8,128)S(1)}, f32[80,1024]{1,0:T(8,128)S(1)}, u32[]{:S(2)}, u32[]{:S(2)}) collective-permute-start(f32[80,1024]{1,0:T(8,128)S(1)} %broadcast_select_fusion), channel_id=1, source_target_pairs={{80,0},{96,16},{112,32},{128,48},{144,64},{160,80},{176,96},{192,1... | collective-permute-start | bytes 983048 | tf_op jit(solution)/shard_map/ppermute | solution.py:15
  398.2 22.5 %collective-permute-start.28 = (f32[80,1024]{1,0:T(8,128)S(1)}, f32[80,1024]{1,0:T(8,128)S(1)}, u32[]{:S(2)}, u32[]{:S(2)}) collective-permute-start(f32[80,1024]{1,0:T(8,128)S(1)} %broadcast_select_fusion), channel_id=1, source_target_pairs={{96,0},{112,16},{128,32},{144,48},{160,64},{176,80},{192,96},{208,... | collective-permute-start | bytes 983048 | tf_op jit(solution)/shard_map/ppermute | solution.py:15
  399.5 25.3 %collective-permute-start.27 = (f32[80,1024]{1,0:T(8,128)S(1)}, f32[80,1024]{1,0:T(8,128)S(1)}, u32[]{:S(2)}, u32[]{:S(2)}) collective-permute-start(f32[80,1024]{1,0:T(8,128)S(1)} %broadcast_select_fusion), channel_id=1, source_target_pairs={{112,0},{128,16},{144,32},{160,48},{176,64},{192,80},{208,96},{224... | collective-permute-start | bytes 983048 | tf_op jit(solution)/shard_map/ppermute | solution.py:15
  400.8 39.0 %collective-permute-start.26 = (f32[80,1024]{1,0:T(8,128)S(1)}, f32[80,1024]{1,0:T(8,128)S(1)}, u32[]{:S(2)}, u32[]{:S(2)}) collective-permute-start(f32[80,1024]{1,0:T(8,128)S(1)} %broadcast_select_fusion), channel_id=1, source_target_pairs={{128,0},{144,16},{160,32},{176,48},{192,64},{208,80},{224,96},{240... | collective-permute-start | bytes 983048 | tf_op jit(solution)/shard_map/ppermute | solution.py:15
  402.2 39.7 %collective-permute-start.25 = (f32[80,1024]{1,0:T(8,128)S(1)}, f32[80,1024]{1,0:T(8,128)S(1)}, u32[]{:S(2)}, u32[]{:S(2)}) collective-permute-start(f32[80,1024]{1,0:T(8,128)S(1)} %broadcast_select_fusion), channel_id=1, source_target_pairs={{0,128},{16,144},{32,160},{48,176},{64,192},{80,208},{96,224},{112... | collective-permute-start | bytes 983048 | tf_op jit(solution)/shard_map/ppermute | solution.py:15
  411.0 32.7 %collective-permute-start.24 = (f32[80,1024]{1,0:T(8,128)S(1)}, f32[80,1024]{1,0:T(8,128)S(1)}, u32[]{:S(2)}, u32[]{:S(2)}) collective-permute-start(f32[80,1024]{1,0:T(8,128)S(1)} %broadcast_select_fusion), channel_id=1, source_target_pairs={{0,112},{16,128},{32,144},{48,160},{64,176},{80,192},{96,208},{112... | collective-permute-start | bytes 983048 | tf_op jit(solution)/shard_map/ppermute | solution.py:15
  420.8 27.3 %collective-permute-start.23 = (f32[80,1024]{1,0:T(8,128)S(1)}, f32[80,1024]{1,0:T(8,128)S(1)}, u32[]{:S(2)}, u32[]{:S(2)}) collective-permute-start(f32[80,1024]{1,0:T(8,128)S(1)} %broadcast_select_fusion), channel_id=1, source_target_pairs={{0,96},{16,112},{32,128},{48,144},{64,160},{80,176},{96,192},{112,... | collective-permute-start | bytes 983048 | tf_op jit(solution)/shard_map/ppermute | solution.py:15
  424.9 34.3 %collective-permute-start.22 = (f32[80,1024]{1,0:T(8,128)S(1)}, f32[80,1024]{1,0:T(8,128)S(1)}, u32[]{:S(2)}, u32[]{:S(2)}) collective-permute-start(f32[80,1024]{1,0:T(8,128)S(1)} %broadcast_select_fusion), channel_id=1, source_target_pairs={{0,80},{16,96},{32,112},{48,128},{64,144},{80,160},{96,176},{112,1... | collective-permute-start | bytes 983048 | tf_op jit(solution)/shard_map/ppermute | solution.py:15
  439.9 29.4 %collective-permute-start.21 = (f32[80,1024]{1,0:T(8,128)S(1)}, f32[80,1024]{1,0:T(8,128)S(1)}, u32[]{:S(2)}, u32[]{:S(2)}) collective-permute-start(f32[80,1024]{1,0:T(8,128)S(1)} %broadcast_select_fusion), channel_id=1, source_target_pairs={{0,64},{16,80},{32,96},{48,112},{64,128},{80,144},{96,160},{112,17... | collective-permute-start | bytes 983048 | tf_op jit(solution)/shard_map/ppermute | solution.py:15
  441.8 27.4 %collective-permute-start.20 = (f32[80,1024]{1,0:T(8,128)S(1)}, f32[80,1024]{1,0:T(8,128)S(1)}, u32[]{:S(2)}, u32[]{:S(2)}) collective-permute-start(f32[80,1024]{1,0:T(8,128)S(1)} %broadcast_select_fusion), channel_id=1, source_target_pairs={{0,48},{16,64},{32,80},{48,96},{64,112},{80,128},{96,144},{112,160... | collective-permute-start | bytes 983048 | tf_op jit(solution)/shard_map/ppermute | solution.py:15
  443.8 29.5 %collective-permute-start.19 = (f32[80,1024]{1,0:T(8,128)S(1)}, f32[80,1024]{1,0:T(8,128)S(1)}, u32[]{:S(2)}, u32[]{:S(2)}) collective-permute-start(f32[80,1024]{1,0:T(8,128)S(1)} %broadcast_select_fusion), channel_id=1, source_target_pairs={{0,32},{16,48},{32,64},{48,80},{64,96},{80,112},{96,128},{112,144}... | collective-permute-start | bytes 983048 | tf_op jit(solution)/shard_map/ppermute | solution.py:15
  448.0 43.0 %collective-permute-start.18 = (f32[80,1024]{1,0:T(8,128)S(1)}, f32[80,1024]{1,0:T(8,128)S(1)}, u32[]{:S(2)}, u32[]{:S(2)}) collective-permute-start(f32[80,1024]{1,0:T(8,128)S(1)} %broadcast_select_fusion), channel_id=1, source_target_pairs={{0,16},{16,32},{32,48},{48,64},{64,80},{80,96},{96,112},{112,128},... | collective-permute-start | bytes 983048 | tf_op jit(solution)/shard_map/ppermute | solution.py:15
  (31 other events, 777.9 us)
where the time goes:
time: 674 us; the launch traced here: 663 us
  other arithmetic  262 us (39%)
  starting transfers between devices  158 us (23%)
  waiting for transfers between devices  124 us (18%)
  matrix products  88.3 us (13%)
  local copies, waits for them, and re-layouts  17 us (3%)
  loops' own time  7.32 us (1%)
    ppermute x36, starting transfers between devices, from_behind(): return lax.ppermute(x, axis, pairs)  158 us
    ppermute x36, waiting for transfers between devices, from_behind(): return lax.ppermute(x, axis, pairs)  124 us
    reduce_sum x160, other arithmetic, eliminate(): pivot = jnp.sum(pivot_row * col_pick)  102 us
    div x160, other arithmetic, eliminate(): pivot_row = pivot_row / pivot  100 us
    dot_general x8, matrix products, shards(): jnp.dot(slab.T, obs_anom, precision=HIGH, preferred_element_type=jnp.floa...  38.8 us
    dot_general x8, matrix products, shards(): jnp.dot(weights, (taper * cross).T, precision=HIGH, preferred_element_typ...  33.4 us
    reduce_sum x160, other arithmetic, eliminate(): pivot_row = jnp.sum(current * row_pick[:, None], axis=0)  21.5 us
    select_n x160, other arithmetic, eliminate(): return jnp.where((row_ids == step)[:, None], pivot_row[None, :], reduced)  14.7 us
  transfers between devices with their start and end apart: 36, of which 13 were waited for; matrix products, arithmetic and copies ran while one was open for 2% of the time, Pallas kernels for 0%

commit v1 on v0

v1 whole, which is shorter than its diff:
```python
import jax
import jax.numpy as jnp
from jax import lax
from jax.experimental import pallas as pl
from jax.experimental.pallas import tpu as pltpu
from jax.sharding import PartitionSpec as P

HIGH = lax.Precision.HIGHEST
F32 = jnp.float32
BF16 = jnp.bfloat16
LOC = 64
MEMBERS = 80
NT = (((1,), (1,)), ((), ()))
NN = (((1,), (0,)), ((), ()))


def split(v):
    hi = v.astype(BF16)
    lo = (v - hi.astype(F32)).astype(BF16)
    return hi, lo


def dot(a, b, dims=NN, precision=None):
    return lax.dot_general(a, b, dims, precision=precision, preferred_element_type=F32)


def pick_kernel(place, state, ox, oy, ol, out):
    gx = lax.axis_index("gx")
    gy = lax.axis_index("gy")
    for b in range(2):
        owned = jnp.logical_and(place[0, b] == gx, place[1, b] == gy)

        @pl.when(owned)
        def _():
            @pl.loop(0, 8)
            def _(c):
                cols = pl.ds(pl.multiple_of(c * 128, 128), 128)
                want = ol[b : b + 1, cols] * 8 + ox[b : b + 1, cols]
                at = jnp.broadcast_to(oy[b : b + 1, cols], (MEMBERS, 128))
                got = jnp.zeros((MEMBERS, 128), F32)
                for row in range(32):
                    cells = state[pl.ds(row, MEMBERS, stride=32), :]
                    moved = jnp.take_along_axis(cells, at, axis=1)
                    got = jnp.where(want == row, moved, got)
                out[b, c] = got

        @pl.when(jnp.logical_not(owned))
        def _():
            out[b] = jnp.zeros((8, MEMBERS, 128), F32)


def invert(m):
    rows = lax.broadcasted_iota(jnp.int32, (MEMBERS, 1), 0)
    lanes = lax.broadcasted_iota(jnp.int32, (1, 128), 1)
    for j in range(0, MEMBERS, 2):
        r0, r1 = m[j : j + 1], m[j + 1 : j + 2]
        a, b, d = r0[:, j : j + 1], r0[:, j + 1 : j + 2], r1[:, j + 1 : j + 2]
        scale = 1.0 / (a * d - b * b)
        i00, i01, i11 = d * scale, -b * scale, a * scale
        c0, c1 = m[:, j : j + 1], m[:, j + 1 : j + 2]
        first, second = lanes == j, lanes == j + 1
        both = jnp.logical_or(first, second)
        r0 = jnp.where(both, jnp.where(first, 1.0, 0.0), r0)
        r1 = jnp.where(both, jnp.where(second, 1.0, 0.0), r1)
        s0 = i00 * r0 + i01 * r1
        s1 = i01 * r0 + i11 * r1
        top, low = rows == j, rows == j + 1
        c0 = jnp.where(top, -1.0, jnp.where(low, 0.0, c0))
        c1 = jnp.where(low, -1.0, jnp.where(top, 0.0, c1))
        rest = jnp.where(jnp.logical_or(both, jnp.logical_or(top, low)), 0.0, m)
        m = rest - c0 * s0 - c1 * s1
    return m


def update_kernel(place, state, obs, ox, oy, ol, value, noise, var, out,
                  held, both, scaled, cast, weights, near_y, col_x, col_y, col_l, taper, hx, sem):
    gx = lax.axis_index("gx")
    gy = lax.axis_index("gy")
    load = pltpu.make_async_copy(state, out, sem)
    load.start()

    def close(b, x, y):
        return jnp.logical_and(jnp.abs(x - place[0, b]) <= 8, jnp.abs(y - place[1, b]) <= 1)

    near = [close(b, gx, gy) for b in range(2)]
    linked = jnp.logical_and(near[1], close(0, place[0, 1], place[1, 1]))
    hx[...] = obs[...]

    def prepare(b):
        for c in range(8):
            cols = slice(c * 128, c * 128 + 128)
            h = hx[b, c]
            o = h - jnp.sum(h, axis=0, keepdims=True) * (1.0 / MEMBERS)
            d = value[b : b + 1, cols] + noise[b, :, cols] - h
            both[0:MEMBERS, cols] = o
            both[MEMBERS : 2 * MEMBERS, cols] = d
            scaled[:, cols] = o * (1.0 / var[b : b + 1, cols])
            three = jnp.concatenate([o, o, o, jnp.zeros((16, 128), F32)], axis=0)
            held[cols, 0:128] = three[0:128].T
            held[cols, 128:256] = three[128:256].T
            for ref, dst in ((ox, col_x), (oy, col_y), (ol, col_l)):
                dst[cols, :] = jnp.broadcast_to(ref[b : b + 1, cols].astype(F32), (128, 128)).T
        gram = dot(both[...], scaled[...], NT, HIGH)
        inner = jnp.concatenate([gram[0:MEMBERS], jnp.zeros((MEMBERS, 48), F32)], axis=1)
        eye = lax.broadcasted_iota(jnp.int32, (MEMBERS, 128), 0) == lax.broadcasted_iota(
            jnp.int32, (MEMBERS, 128), 1
        )
        inner = inner + jnp.where(eye, MEMBERS - 1.0, 0.0)
        inverse = invert(inner)
        factor = dot(gram[MEMBERS : 2 * MEMBERS], inverse[:, 0:MEMBERS], NN, HIGH)
        w = both[MEMBERS : 2 * MEMBERS] - dot(factor, both[0:MEMBERS], NN, HIGH)
        w = w * (1.0 / var[b : b + 1, :])
        hi, lo = split(w)
        weights[0:MEMBERS] = hi
        weights[MEMBERS : 2 * MEMBERS] = lo
        lane = lax.broadcasted_iota(jnp.int32, (1, 128), 1)
        mesh_y = (gy * 128 + lane).astype(F32) - (place[1, b] * 128).astype(F32)

        @pl.loop(0, 8)
        def _(c):
            cols = pl.ds(pl.multiple_of(c * 128, 128), 128)
            dy = mesh_y - col_y[cols, :]
            near_y[cols, :] = 1.0 - dy * dy * (1.0 / (LOC * LOC))
            for level in range(4):
                gap = jnp.abs(level - col_l[cols, :])
                factor_l = (1.0 / (1.0 + gap)) * (1.0 / (MEMBERS - 1))
                for half in range(2):
                    part = held[cols, half * 128 : half * 128 + 128] * factor_l
                    hi, lo = split(part)
                    if half == 1:
                        hi = jnp.where(lane < 32, hi.astype(F32), lo.astype(F32)).astype(BF16)
                    cast[level, cols, half * 128 : half * 128 + 128] = hi

    def gain(values, level, taper_at):
        mean = jnp.sum(values, axis=0, keepdims=True) * (1.0 / MEMBERS)
        hi, lo = split(values - mean)
        right = jnp.concatenate([hi, lo, hi, jnp.zeros((16, values.shape[1]), BF16)], axis=0)
        total = jnp.zeros((2 * MEMBERS, values.shape[1]), F32)
        rest = jnp.zeros((MEMBERS, values.shape[1]), F32)
        for part in range(4):
            span = slice(part * 256, part * 256 + 256)
            cross = dot(cast[level, span, :], right)
            hi, lo = split(cross * taper_at(span))
            total = total + dot(weights[:, span], hi)
            rest = rest + dot(weights[0:MEMBERS, span], lo)
        return total[0:MEMBERS] + total[MEMBERS : 2 * MEMBERS] + rest

    def move_state(b):
        @pl.loop(0, 4)
        def _(pair):
            for half in range(2):
                x = (gx * 8 + pair * 2 + half).astype(F32) - (place[0, b] * 8).astype(F32)

                @pl.loop(0, 8)
                def _(c):
                    cols = pl.ds(pl.multiple_of(c * 128, 128), 128)
                    dx = x - col_x[cols, :]
                    t = jnp.maximum(near_y[cols, :] - dx * dx * (1.0 / (LOC * LOC)), 0.0)
                    taper[cols, half * 128 : half * 128 + 128] = t * t

            @pl.loop(0, 4)
            def _(level):
                rows = [pl.ds(level * 8 + pair * 2 + half, MEMBERS, stride=32) for half in range(2)]
                cells = [out[r, :] for r in rows]
                change = gain(jnp.concatenate(cells, axis=1), level, lambda span: taper[span, :])
                for half in range(2):
                    out[rows[half], :] = cells[half] + change[:, half * 128 : half * 128 + 128]

    def move_obs():
        @pl.loop(0, 8)
        def _(c):
            cols = pl.ds(pl.multiple_of(c * 128, 128), 128)
            x = (ox[1:2, cols] + (place[0, 1] - place[0, 0]) * 8).astype(F32)
            y = (oy[1:2, cols] + (place[1, 1] - place[1, 0]) * 128).astype(F32)
            lev = ol[1:2, cols].astype(F32)

            def taper_at(span):
                dx = x - col_x[span, :]
                dy = y - col_y[span, :]
                t = jnp.maximum(1.0 - (dx * dx + dy * dy) * (1.0 / (LOC * LOC)), 0.0)
                gap = jnp.abs(col_l[span, :] - lev)
                own = jnp.abs(col_l[span, :])
                return t * t * (1.0 + own) / (1.0 + gap)

            h = hx[1, c]
            hx[1, c] = h + gain(h, 0, taper_at)

    @pl.when(jnp.logical_or(near[0], linked))
    def _():
        prepare(0)

    load.wait()

    @pl.when(near[0])
    def _():
        move_state(0)

    @pl.when(linked)
    def _():
        move_obs()

    @pl.when(near[1])
    def _():
        prepare(1)
        move_state(1)


VMEM = pl.BlockSpec(memory_space=pltpu.VMEM)
SMEM = pl.BlockSpec(memory_space=pltpu.SMEM)
ANY = pl.BlockSpec(memory_space=pl.ANY)


def pick(place, state, ox, oy, ol):
    return pl.pallas_call(
        pick_kernel,
        out_shape=jax.ShapeDtypeStruct((2, 8, MEMBERS, 128), F32),
        in_specs=[SMEM, VMEM, VMEM, VMEM, VMEM],
        out_specs=VMEM,
        compiler_params=pltpu.CompilerParams(vmem_limit_bytes=48 * 2**20),
    )(place, state, ox, oy, ol)


def update(place, state, obs, ox, oy, ol, value, noise, var):
    S = pltpu.VMEM
    return pl.pallas_call(
        update_kernel,
        out_shape=jax.ShapeDtypeStruct(state.shape, F32),
        in_specs=[SMEM, ANY] + [VMEM] * 7,
        out_specs=VMEM,
        scratch_shapes=[
            S((1024, 256), F32),
            S((160, 1024), F32),
            S((MEMBERS, 1024), F32),
            S((4, 1024, 256), BF16),
            S((160, 1024), BF16),
            S((1024, 128), F32),
            S((1024, 128), F32),
            S((1024, 128), F32),
            S((1024, 128), F32),
            S((1024, 256), F32),
            S((2, 8, MEMBERS, 128), F32),
            pltpu.SemaphoreType.DMA,
        ],
        compiler_params=pltpu.CompilerParams(vmem_limit_bytes=56 * 2**20),
    )(place, state, obs, ox, oy, ol, value, noise, var)


MESH = pl.DeviceIdType.MESH

def spread_kernel(piece, out, pair_buf, acc, ring_buf, z_src, z_buf,
                  s0s, s0r, s1s, s1r, s2s, s2r, s3s, s3r, s4s, s4r):
    gx = lax.axis_index("gx")
    gy = lax.axis_index("gy")
    yy = gx // 4
    zh = gx % 4
    zl = gy // 8
    xx = (gy // 2) % 4
    core = gy % 2
    other = 1 - core
    q = yy * 4 + xx
    z = zh * 2 + zl

    def dev_xy(t):
        return ((t // 4) * 4 + zh, zl * 8 + (t % 4) * 2 + core)

    def dev_z(t):
        return (yy * 4 + t // 2, (t % 2) * 8 + xx * 2 + core)

    mate = (gx, zl * 8 + xx * 2 + other)

    barrier = pltpu.get_barrier_semaphore()

    @pl.loop(1, 16)
    def _(d):
        pl.semaphore_signal(barrier, inc=1, device_id=dev_xy((q + d) % 16), device_id_type=MESH)

    @pl.loop(1, 8)
    def _(d):
        pl.semaphore_signal(barrier, inc=1, device_id=dev_z((z + d) % 8), device_id_type=MESH)

    pl.semaphore_signal(barrier, inc=1, device_id=mate, device_id_type=MESH)
    pl.semaphore_wait(barrier, 23)

    def c0(t):
        return pltpu.make_async_remote_copy(
            src_ref=piece.at[other, t], dst_ref=pair_buf.at[t], send_sem=s0s.at[t], recv_sem=s0r.at[t],
            device_id=mate, device_id_type=MESH)

    def c1(t, slot):
        return pltpu.make_async_remote_copy(
            src_ref=acc.at[t], dst_ref=ring_buf.at[slot], send_sem=s1s.at[t], recv_sem=s1r.at[slot],
            device_id=dev_xy(t), device_id_type=MESH)

    def c2(t, slot):
        return pltpu.make_async_remote_copy(
            src_ref=z_src, dst_ref=z_buf.at[slot], send_sem=s2s.at[t], recv_sem=s2r.at[slot],
            device_id=dev_z(t), device_id_type=MESH)

    def c3(t, slot):
        return pltpu.make_async_remote_copy(
            src_ref=out.at[core, slot], dst_ref=out.at[core, slot], send_sem=s3s.at[t], recv_sem=s3r.at[slot],
            device_id=dev_xy(t), device_id_type=MESH)

    def c4(w, slot):
        return pltpu.make_async_remote_copy(
            src_ref=out.at[w, slot], dst_ref=out.at[w, slot], send_sem=s4s.at[slot], recv_sem=s4r.at[slot],
            device_id=mate, device_id_type=MESH)

    @pl.loop(1, 17)
    def _(d):
        c0((q + d) % 16).start()

    @pl.loop(1, 16)
    def _(d):
        t = (q + d) % 16
        c0(t).wait_recv()
        acc[t] = piece[core, t] + pair_buf[t]
        c1(t, q).start()

    c0(q).wait_recv()
    z_src[...] = piece[core, q] + pair_buf[q]

    @pl.loop(1, 16)
    def _(d):
        t = (q + 16 - d) % 16
        c1(t, t).wait_recv()
        z_src[...] += ring_buf[t]

    @pl.loop(1, 8)
    def _(d):
        c2((z + d) % 8, z).start()

    out[core, q] = z_src[...]

    @pl.loop(1, 8)
    def _(d):
        t = (z + 8 - d) % 8
        c2(t, t).wait_recv()
        out[core, q] += z_buf[t]

    @pl.loop(1, 16)
    def _(d):
        c3((q + d) % 16, q).start()

    c4(core, q).start()

    @pl.loop(1, 16)
    def _(d):
        t = (q + 16 - d) % 16
        c3(t, t).wait_recv()
        c4(core, t).start()

    @pl.loop(0, 16)
    def _(d):
        c4(other, (q + 16 - d) % 16).wait_recv()

    @pl.loop(0, 16)
    def _(t):
        c0(t).wait_send()
        c4(core, t).wait_send()

    @pl.loop(1, 16)
    def _(d):
        t = (q + d) % 16
        c1(t, q).wait_send()
        c3(t, q).wait_send()

    @pl.loop(1, 8)
    def _(d):
        c2((z + d) % 8, z).wait_send()


def spread(piece):
    D = pltpu.SemaphoreType.DMA
    return pl.pallas_call(
        spread_kernel,
        out_shape=jax.ShapeDtypeStruct((2, 16, 40, 128), jnp.float32),
        in_specs=[pl.BlockSpec(memory_space=pltpu.VMEM)],
        out_specs=pl.BlockSpec(memory_space=pltpu.VMEM),
        scratch_shapes=[
            pltpu.VMEM((16, 40, 128), jnp.float32),
            pltpu.VMEM((16, 40, 128), jnp.float32),
            pltpu.VMEM((16, 40, 128), jnp.float32),
            pltpu.VMEM((40, 128), jnp.float32),
            pltpu.VMEM((8, 40, 128), jnp.float32),
            D((16,)), D((16,)), D((16,)), D((16,)), D((8,)), D((8,)), D((16,)), D((16,)), D((16,)), D((16,)),
        ],
        compiler_params=pltpu.CompilerParams(collective_id=0, has_side_effects=True),
    )(piece)


def shards(ensemble, obs_x, obs_y, obs_level, owner_row, owner_col, obs_value, obs_noise, obs_var):
    place = jnp.stack([owner_row, owner_col])
    state = ensemble.reshape(-1, ensemble.shape[3])
    piece = pick(place, state, obs_x, obs_y, obs_level)
    obs = spread(piece.reshape(2, 16, 40, 128)).reshape(2, 8, MEMBERS, 128)
    out = update(place, state, obs, obs_x, obs_y, obs_level, obs_value, obs_noise, obs_var)
    return out.reshape(ensemble.shape)


def solution(mesh):
    in_specs = (P(None, None, "gx", "gy"), P(), P(), P(), P(), P(), P(), P(), P())
    out_specs = P(None, None, "gx", "gy")
    return jax.shard_map(shards, mesh=mesh, in_specs=in_specs, out_specs=out_specs, check_vma=False)
```

time: 674 us -> 78.4 us (0.12)
  the two profiles are of different devices: /device:TPU:74 before, /device:TPU:7 now
where the time goes in v1:
time: 78.4 us; the launch traced here: 78.1 us
  Pallas kernels  73 us (93%)
  local copies, waits for them, and re-layouts  4.24 us (5%)
    pallas_call x1, Pallas kernels, spread(): pl.pallas_call(spread_kernel, out_shape=jax.ShapeDtypeStruct((2, 16, 40,...  42.7 us
    pallas_call x1, Pallas kernels, update(): pl.pallas_call(update_kernel, out_shape=jax.ShapeDtypeStruct(state.shape,...  29.7 us
    unnamed x12, local copies, waits for them, and re-layouts  4.24 us

profile of v1, /device:TPU:7, one launch (start us, length us, event | category | flops | bytes accessed | tf_op | source)
XLA Modules:
  0.0 78.1 jit_solution(7413423834538189988)
XLA Ops:
  0.0 0.7 pad_add_fusion.place
  0.7 0.0 copy-start
  0.7 1.3 %copy-done = f32[80,4,8,128]{3,2,1,0:T(8,128)S(1)} copy-done((f32[80,4,8,128]{3,2,1,0:T(8,128)S(1)}, f32[80,4,8,128]{3,2,1,0:T(8,128)}, u32[]{:S(2)}) %copy-start) | copy-done | bytes 1310744
  2.0 0.0 copy-start.2
  2.0 0.7 copy-done.2
  2.7 0.0 copy-start.3
  2.7 0.7 copy-done.3
  3.4 0.0 copy-start.4
  3.4 0.7 copy-done.4
  4.1 0.0 copy-start.5
  4.1 0.6 shard_map.91
  4.7 0.0 copy-start.1
  4.7 0.8 %copy-done.1 = f32[2,8,80,128]{3,2,1,0:T(8,128)} copy-done((f32[2,8,80,128]{3,2,1,0:T(8,128)}, f32[2,8,80,128]{3,2,1,0:T(8,128)S(1)}, u32[]{:S(2)}) %copy-start.1) | copy-done | bytes 655384
  5.6 42.7 %shard_map.92 = f32[2,16,40,128]{3,2,1,0:T(8,128)} custom-call(f32[2,16,40,128]{3,2,1,0:T(8,128)} %bitcast.8), custom_call_target="tpu_custom_call" | custom-call | tf_op jit(solution)/shard_map/pallas_call | solution.py:375
  48.2 0.0 copy-done.5
  48.2 29.7 %shard_map.93 = f32[2560,128]{1,0:T(8,128)} custom-call(s32[2,2]{1,0:T(2,128)} %copy-done.5, f32[2560,128]{1,0:T(8,128)} %bitcast.6, f32[2,8,80,128]{3,2,1,0:T(8,128)} %bitcast.9, s32[2,1024]{1,0:T(2,128)} %ox.3, s32[2,1024]{1,0:T(2,128)} %oy.3, s32[2,1024]{1,0:T(2,128)} %ol.3, f32[2,1024]{1,0:T(2,128)} %value.1, f32[2,80,1024]{2,1,0:T(8,128)} %noise.1, ...), custom_call_target="tpu_custom_call" | custom-call | tf_op jit(solution)/shard_map/pallas_call | solution.py:225
Async XLA Ops:
  0.7 1.3 %copy-start = (f32[80,4,8,128]{3,2,1,0:T(8,128)S(1)}, f32[80,4,8,128]{3,2,1,0:T(8,128)}, u32[]{:S(2)}) copy-start(f32[80,4,8,128]{3,2,1,0:T(8,128)} %param.9) | copy-start | bytes 3932164
  2.0 0.7 copy-start.2
  2.7 0.7 copy-start.3
  3.4 0.7 copy-start.4
  4.1 44.1 %copy-start.5 = (s32[2,2]{1,0:T(2,128)}, s32[2,2]{1,0:T(2,128)S(1)}, u32[]{:S(2)}) copy-start(s32[2,2]{1,0:T(2,128)S(1)} %pad_add_fusion.place) | copy-start | bytes 52
  4.7 0.8 %copy-start.1 = (f32[2,8,80,128]{3,2,1,0:T(8,128)}, f32[2,8,80,128]{3,2,1,0:T(8,128)S(1)}, u32[]{:S(2)}) copy-start(f32[2,8,80,128]{3,2,1,0:T(8,128)S(1)} %shard_map.91) | copy-start | bytes 1966084

commit v2 on v1

v2 whole, which is shorter than its diff:
```python
import jax
import jax.numpy as jnp
from jax import lax
from jax.experimental import pallas as pl
from jax.experimental.pallas import tpu as pltpu
from jax.sharding import PartitionSpec as P

HIGH = lax.Precision.HIGHEST
F32 = jnp.float32
BF16 = jnp.bfloat16
LOC = 64
MEMBERS = 80
NT = (((1,), (1,)), ((), ()))
NN = (((1,), (0,)), ((), ()))


def split(v):
    hi = v.astype(BF16)
    lo = (v - hi.astype(F32)).astype(BF16)
    return hi, lo


def dot(a, b, dims=NN, precision=None):
    return lax.dot_general(a, b, dims, precision=precision, preferred_element_type=F32)


def pick_kernel(row_in, col_in, state, ox_in, oy_in, ol_in, out, row, col, ox, oy, ol, cells, sem, sem_cells):
    gx = lax.axis_index("gx")
    gy = lax.axis_index("gy")
    small = [(row_in, row), (col_in, col), (ox_in, ox), (oy_in, oy), (ol_in, ol)]
    small = [pltpu.make_async_copy(src, dst, sem.at[i]) for i, (src, dst) in enumerate(small)]
    for copy in small:
        copy.start()
    small[0].wait()
    small[1].wait()
    owned = [jnp.logical_and(row[b] == gx, col[b] == gy) for b in range(2)]

    @pl.when(jnp.logical_or(owned[0], owned[1]))
    def _():
        @pl.loop(0, 32)
        def _(r):
            pltpu.make_async_copy(state.at[:, r], cells.at[r], sem_cells).start()

    for copy in small[2:]:
        copy.wait()

    @pl.when(jnp.logical_or(owned[0], owned[1]))
    def _():
        pltpu.make_async_copy(cells, cells, sem_cells).wait()

    for b in range(2):

        @pl.when(owned[b])
        def _():
            @pl.loop(0, 8)
            def _(c):
                cols = pl.ds(pl.multiple_of(c * 128, 128), 128)
                want = jnp.broadcast_to(ol[b : b + 1, cols] * 8 + ox[b : b + 1, cols], (8, 128))
                at = jnp.broadcast_to(oy[b : b + 1, cols], (8, 128))
                for k in range(0, MEMBERS, 8):
                    got = jnp.zeros((8, 128), F32)
                    for r in range(32):
                        moved = jnp.take_along_axis(cells[r, k : k + 8], at, axis=1, mode="promise_in_bounds")
                        got = jnp.where(want == r, moved, got)
                    out[b, c, k : k + 8] = got

        @pl.when(jnp.logical_not(owned[b]))
        def _():
            out[b] = jnp.zeros((8, MEMBERS, 128), F32)


def inverse_of(a, keep):
    eye = jnp.where(
        lax.broadcasted_iota(jnp.int32, a.shape, 0) == lax.broadcasted_iota(jnp.int32, a.shape, 1), 1.0, 0.0
    )
    top = jnp.max(jnp.sum(jnp.abs(a), axis=1, keepdims=True), axis=0, keepdims=True)
    scale = 2.0 / (top + (MEMBERS - 1.0))
    r = eye - scale * a
    x = scale * (eye + r)
    for _ in range(5):
        r = dot(r, r, NN, HIGH)
        x = x + dot(x, r, NN, HIGH)

    keep[0] = x
    keep[1] = r

    def more(held):
        return jnp.logical_and(held[0] > 1e-4, held[1] < 40)

    def rest(held):
        r = dot(keep[1], keep[1], NN, HIGH)
        keep[0] = keep[0] + dot(keep[0], r, NN, HIGH)
        keep[1] = r
        return jnp.max(jnp.abs(r)), held[1] + 1

    _, count = lax.while_loop(more, rest, (jnp.max(jnp.abs(r)), jnp.int32(0)))

    @pl.when(count > 0)
    def _():
        x = keep[0]
        keep[0] = x + dot(x, eye - dot(a, x, NN, HIGH), NN, HIGH)

    return keep[0]


def update_kernel(row_in, col_in, state, obs, ox_in, oy_in, ol_in, value_in, noise_in, var_in, out,
                  row, col, ox, oy, ol, value, var, cells, hx, noises, both, scaled, cast, weights, near_y, col_x, col_y, col_f, taper, keep, gain_hi, gain_lo,
                  sem_in, sem_obs, sem_out):
    gx = lax.axis_index("gx")
    gy = lax.axis_index("gy")
    small = [(row_in, row), (col_in, col), (ox_in, ox), (oy_in, oy), (ol_in, ol), (value_in, value), (var_in, var)]
    small += [(obs, hx), (noise_in, noises)]
    small = [pltpu.make_async_copy(src, dst, sem_obs.at[i]) for i, (src, dst) in enumerate(small)]
    for copy in small[:2]:
        copy.start()
    for copy in small[:2]:
        copy.wait()

    def close(b, x, y):
        return jnp.logical_and(jnp.abs(x - row[b]) <= 8, jnp.abs(y - col[b]) <= 1)

    near = [close(b, gx, gy) for b in range(2)]
    linked = jnp.logical_and(near[1], close(0, row[1], col[1]))
    any_near = jnp.logical_or(near[0], near[1])
    whole = pltpu.make_async_copy(state, out, sem_out)
    all_in = pltpu.make_async_copy(cells, cells, sem_in)
    all_out = pltpu.make_async_copy(cells, cells, sem_out)

    def fetch(r):
        return pltpu.make_async_copy(state.at[:, r], cells.at[r], sem_in)

    def store(r):
        return pltpu.make_async_copy(cells.at[r], out.at[:, r], sem_out)

    @pl.when(any_near)
    def _():
        for copy in small[2:]:
            copy.start()

        @pl.loop(0, 32)
        def _(r):
            fetch(r).start()

        for copy in small[2:]:
            copy.wait()

    @pl.when(jnp.logical_not(any_near))
    def _():
        whole.start()
        whole.wait()

    def prepare(b):
        lane = lax.broadcasted_iota(jnp.int32, (1, 128), 1)
        mesh_y = (gy * 128 + lane - col[b] * 128).astype(F32) * (1.0 / LOC)

        @pl.loop(0, 8)
        def _(c):
            cols = pl.ds(pl.multiple_of(c * 128, 128), 128)
            h = hx[b, c]
            inv = 1.0 / var[b : b + 1, cols]
            o = h - jnp.sum(h, axis=0, keepdims=True) * (1.0 / MEMBERS)
            d = value[b : b + 1, cols] + noises[b, :, cols] - h
            both[0:MEMBERS, cols] = o
            both[MEMBERS : 2 * MEMBERS, cols] = d
            scaled[:, cols] = o * inv
            lev = ol[b : b + 1, cols].astype(F32)
            extra = [ox[b : b + 1, cols].astype(F32) * (1.0 / LOC), oy[b : b + 1, cols].astype(F32) * (1.0 / LOC)]
            for level in range(4):
                extra.append(1.0 / ((1.0 + jnp.abs(level - lev)) * (MEMBERS - 1)))
            extra.append(jnp.zeros((42, 128), F32))
            turned = jnp.concatenate([o] + extra, axis=0).T
            x_at = jnp.broadcast_to(turned[:, 80:81], (128, 128))
            y_at = jnp.broadcast_to(turned[:, 81:82], (128, 128))
            col_x[cols, :] = x_at
            col_y[cols, :] = y_at
            dy = mesh_y - y_at
            near_y[cols, :] = 1.0 - dy * dy
            turned_o = jnp.where(lane < MEMBERS, turned, 0.0)
            first = turned_o + jnp.where(lane >= MEMBERS, pltpu.roll(turned, MEMBERS, 1), 0.0)
            second = jnp.where(lane < 32, pltpu.roll(turned, MEMBERS, 1), 0.0) + pltpu.roll(turned_o, 32, 1)
            for level in range(5):
                if level < 4:
                    f_at = jnp.broadcast_to(turned[:, 82 + level : 83 + level], (128, 128))
                    col_f[level, cols, :] = f_at
                    left, right = first * f_at, second * f_at
                else:
                    left, right = first, second
                hi = right.astype(BF16).astype(F32)
                cast[level, cols, 0:128] = left.astype(BF16)
                cast[level, cols, 128:256] = jnp.where(lane < 32, hi, right - hi).astype(BF16)

        gram = dot(both[...], scaled[...], NT, HIGH)
        inner = gram[0:MEMBERS]
        eye = lax.broadcasted_iota(jnp.int32, (MEMBERS, MEMBERS), 0) == lax.broadcasted_iota(
            jnp.int32, (MEMBERS, MEMBERS), 1
        )
        trace = jnp.sum(jnp.sum(jnp.where(eye, inner, 0.0), axis=1, keepdims=True), axis=0, keepdims=True)
        inner = inner + jnp.where(eye, MEMBERS - 1.0, 0.0) + trace * (1.0 / MEMBERS / MEMBERS)
        inverse = inverse_of(inner, keep)
        factor = dot(gram[MEMBERS : 2 * MEMBERS], inverse, NN, HIGH)
        w = both[MEMBERS : 2 * MEMBERS] - dot(factor, both[0:MEMBERS], NN, HIGH)
        w = w * (1.0 / var[b : b + 1, :])
        hi, lo = split(w)
        weights[0:MEMBERS] = hi
        weights[MEMBERS : 2 * MEMBERS] = lo

    def spread_of(values):
        mean = jnp.sum(values, axis=0, keepdims=True) * (1.0 / MEMBERS)
        hi, lo = split(values - mean)
        return jnp.concatenate([hi, lo, hi, jnp.zeros((16, values.shape[1]), BF16)], axis=0)

    def gain(values, level, taper_at, slot=0):
        right = spread_of(values)
        wide = values.shape[1]
        for part in range(4):
            span = slice(part * 256, part * 256 + 256)
            cross = dot(cast[level, span, :], right)
            hi, lo = split(cross * taper_at(span))
            gain_hi[slot, span, 0:wide] = hi
            gain_lo[slot, span, 0:wide] = lo
        total = dot(weights[...], gain_hi[slot, :, 0:wide])
        rest = dot(weights[0:MEMBERS], gain_lo[slot, :, 0:wide])
        return total[0:MEMBERS] + total[MEMBERS : 2 * MEMBERS] + rest

    def move_state(b, last):
        @pl.loop(0, 4)
        def _(pair):
            for half in range(2):
                x = (gx * 8 + pair * 2 + half - row[b] * 8).astype(F32) * (1.0 / LOC)

                @pl.loop(0, 8)
                def _(c):
                    cols = pl.ds(pl.multiple_of(c * 128, 128), 128)
                    dx = x - col_x[cols, :]
                    t = jnp.maximum(near_y[cols, :] - dx * dx, 0.0)
                    taper[cols, half * 128 : half * 128 + 128] = t * t

            before = []
            for level in range(4):
                before.append([cells[level * 8 + pair * 2 + half] for half in range(2)])
            after = []
            for level in range(4):
                change = gain(jnp.concatenate(before[level], axis=1), level, lambda span: taper[span, :], level % 2)
                after.append([before[level][half] + change[:, half * 128 : half * 128 + 128] for half in range(2)])
            for level in range(4):
                for half in range(2):
                    cells[level * 8 + pair * 2 + half] = after[level][half]
            for level in range(4):
                for half in range(2):
                    r = level * 8 + pair * 2 + half
                    if last is True:
                        store(r).start()
                    else:
                        pl.when(last)(store(r).start)

    def move_obs():
        @pl.loop(0, 8)
        def _(c):
            cols = pl.ds(pl.multiple_of(c * 128, 128), 128)
            x = (ox[1:2, cols] + (row[1] - row[0]) * 8).astype(F32) * (1.0 / LOC)
            y = (oy[1:2, cols] + (col[1] - col[0]) * 128).astype(F32) * (1.0 / LOC)
            lev = ol[1:2, cols]

            def taper_at(span):
                dx = x - col_x[span, :]
                dy = y - col_y[span, :]
                t = jnp.maximum(1.0 - (dx * dx + dy * dy), 0.0)
                f = col_f[3, span, :]
                for level in range(3):
                    f = jnp.where(lev == level, col_f[level, span, :], f)
                return t * t * f

            h = hx[1, c]
            hx[1, c] = h + gain(h, 4, taper_at)

    @pl.when(jnp.logical_or(near[0], linked))
    def _():
        prepare(0)

    @pl.when(any_near)
    def _():
        all_in.wait()

    @pl.when(near[0])
    def _():
        move_state(0, jnp.logical_not(near[1]))

    @pl.when(linked)
    def _():
        move_obs()

    @pl.when(near[1])
    def _():
        prepare(1)
        move_state(1, True)

    @pl.when(any_near)
    def _():
        all_out.wait()


VMEM = pl.BlockSpec(memory_space=pltpu.VMEM)
SMEM = pl.BlockSpec(memory_space=pltpu.SMEM)
ANY = pl.BlockSpec(memory_space=pl.ANY)


def pick(row, col, state, ox, oy, ol):
    return pl.pallas_call(
        pick_kernel,
        out_shape=jax.ShapeDtypeStruct((2, 8, MEMBERS, 128), F32),
        in_specs=[ANY] * 6,
        out_specs=VMEM,
        scratch_shapes=[
            pltpu.SMEM((2,), jnp.int32),
            pltpu.SMEM((2,), jnp.int32),
            pltpu.VMEM((2, 1024), jnp.int32),
            pltpu.VMEM((2, 1024), jnp.int32),
            pltpu.VMEM((2, 1024), jnp.int32),
            pltpu.VMEM((32, MEMBERS, 128), F32),
            pltpu.SemaphoreType.DMA((5,)),
            pltpu.SemaphoreType.DMA,
        ],
        compiler_params=pltpu.CompilerParams(vmem_limit_bytes=60 * 2**20),
    )(row, col, state, ox, oy, ol)


def update(row, col, state, obs, ox, oy, ol, value, noise, var):
    S = pltpu.VMEM
    return pl.pallas_call(
        update_kernel,
        out_shape=jax.ShapeDtypeStruct(state.shape, F32),
        in_specs=[ANY] * 10,
        out_specs=ANY,
        scratch_shapes=[
            pltpu.SMEM((2,), jnp.int32),
            pltpu.SMEM((2,), jnp.int32),
            S((2, 1024), jnp.int32),
            S((2, 1024), jnp.int32),
            S((2, 1024), jnp.int32),
            S((2, 1024), F32),
            S((2, 1024), F32),
            S((32, MEMBERS, 128), F32),
            S((2, 8, MEMBERS, 128), F32),
            S((2, MEMBERS, 1024), F32),
            S((160, 1024), F32),
            S((MEMBERS, 1024), F32),
            S((5, 1024, 256), BF16),
            S((160, 1024), BF16),
            S((1024, 128), F32),
            S((1024, 128), F32),
            S((1024, 128), F32),
            S((4, 1024, 128), F32),
            S((1024, 256), F32),
            S((2, MEMBERS, MEMBERS), F32),
            S((2, 1024, 256), BF16),
            S((2, 1024, 256), BF16),
            pltpu.SemaphoreType.DMA,
            pltpu.SemaphoreType.DMA((9,)),
            pltpu.SemaphoreType.DMA,
        ],
        compiler_params=pltpu.CompilerParams(vmem_limit_bytes=60 * 2**20),
    )(row, col, state, obs, ox, oy, ol, value, noise, var)


MESH = pl.DeviceIdType.MESH

def spread_kernel(piece, out, pair_buf, acc, ring_buf, z_src, z_buf,
                  s0s, s0r, s1s, s1r, s2s, s2r, s3s, s3r, s4s, s4r):
    gx = lax.axis_index("gx")
    gy = lax.axis_index("gy")
    yy = gx // 4
    zh = gx % 4
    zl = gy // 8
    xx = (gy // 2) % 4
    core = gy % 2
    other = 1 - core
    q = yy * 4 + xx
    z = zh * 2 + zl

    def dev_xy(t):
        return ((t // 4) * 4 + zh, zl * 8 + (t % 4) * 2 + core)

    def dev_z(t):
        return (yy * 4 + t // 2, (t % 2) * 8 + xx * 2 + core)

    mate = (gx, zl * 8 + xx * 2 + other)

    barrier = pltpu.get_barrier_semaphore()

    @pl.loop(1, 16)
    def _(d):
        pl.semaphore_signal(barrier, inc=1, device_id=dev_xy((q + d) % 16), device_id_type=MESH)

    @pl.loop(1, 8)
    def _(d):
        pl.semaphore_signal(barrier, inc=1, device_id=dev_z((z + d) % 8), device_id_type=MESH)

    pl.semaphore_signal(barrier, inc=1, device_id=mate, device_id_type=MESH)
    pl.semaphore_wait(barrier, 23)

    def c0(t):
        return pltpu.make_async_remote_copy(
            src_ref=piece.at[other, t], dst_ref=pair_buf.at[t], send_sem=s0s.at[t], recv_sem=s0r.at[t],
            device_id=mate, device_id_type=MESH)

    def c1(t, slot):
        return pltpu.make_async_remote_copy(
            src_ref=acc.at[t], dst_ref=ring_buf.at[slot], send_sem=s1s.at[t], recv_sem=s1r.at[slot],
            device_id=dev_xy(t), device_id_type=MESH)

    def c2(t, slot):
        return pltpu.make_async_remote_copy(
            src_ref=z_src, dst_ref=z_buf.at[slot], send_sem=s2s.at[t], recv_sem=s2r.at[slot],
            device_id=dev_z(t), device_id_type=MESH)

    def c3(t, slot):
        return pltpu.make_async_remote_copy(
            src_ref=out.at[core, slot], dst_ref=out.at[core, slot], send_sem=s3s.at[t], recv_sem=s3r.at[slot],
            device_id=dev_xy(t), device_id_type=MESH)

    def c4(w, slot):
        return pltpu.make_async_remote_copy(
            src_ref=out.at[w, slot], dst_ref=out.at[w, slot], send_sem=s4s.at[slot], recv_sem=s4r.at[slot],
            device_id=mate, device_id_type=MESH)

    @pl.loop(1, 17)
    def _(d):
        c0((q + d) % 16).start()

    @pl.loop(1, 16)
    def _(d):
        t = (q + d) % 16
        c0(t).wait_recv()
        acc[t] = piece[core, t] + pair_buf[t]
        c1(t, q).start()

    c0(q).wait_recv()
    z_src[...] = piece[core, q] + pair_buf[q]

    @pl.loop(1, 16)
    def _(d):
        t = (q + 16 - d) % 16
        c1(t, t).wait_recv()
        z_src[...] += ring_buf[t]

    @pl.loop(1, 8)
    def _(d):
        c2((z + d) % 8, z).start()

    out[core, q] = z_src[...]

    @pl.loop(1, 8)
    def _(d):
        t = (z + 8 - d) % 8
        c2(t, t).wait_recv()
        out[core, q] += z_buf[t]

    @pl.loop(1, 16)
    def _(d):
        c3((q + d) % 16, q).start()

    c4(core, q).start()

    @pl.loop(1, 16)
    def _(d):
        t = (q + 16 - d) % 16
        c3(t, t).wait_recv()
        c4(core, t).start()

    @pl.loop(0, 16)
    def _(d):
        c4(other, (q + 16 - d) % 16).wait_recv()

    @pl.loop(0, 16)
    def _(t):
        c0(t).wait_send()
        c4(core, t).wait_send()

    @pl.loop(1, 16)
    def _(d):
        t = (q + d) % 16
        c1(t, q).wait_send()
        c3(t, q).wait_send()

    @pl.loop(1, 8)
    def _(d):
        c2((z + d) % 8, z).wait_send()


def spread(piece):
    D = pltpu.SemaphoreType.DMA
    return pl.pallas_call(
        spread_kernel,
        out_shape=jax.ShapeDtypeStruct((2, 16, 40, 128), jnp.float32),
        in_specs=[pl.BlockSpec(memory_space=pltpu.VMEM)],
        out_specs=pl.BlockSpec(memory_space=pltpu.VMEM),
        scratch_shapes=[
            pltpu.VMEM((16, 40, 128), jnp.float32),
            pltpu.VMEM((16, 40, 128), jnp.float32),
            pltpu.VMEM((16, 40, 128), jnp.float32),
            pltpu.VMEM((40, 128), jnp.float32),
            pltpu.VMEM((8, 40, 128), jnp.float32),
            D((16,)), D((16,)), D((16,)), D((16,)), D((8,)), D((8,)), D((16,)), D((16,)), D((16,)), D((16,)),
        ],
        compiler_params=pltpu.CompilerParams(collective_id=0, has_side_effects=True),
    )(piece)


def shards(ensemble, obs_x, obs_y, obs_level, owner_row, owner_col, obs_value, obs_noise, obs_var):
    cells = ensemble.reshape(MEMBERS, 32, 128)
    piece = pick(owner_row, owner_col, cells, obs_x, obs_y, obs_level)
    obs = spread(piece.reshape(2, 16, 40, 128)).reshape(2, 8, MEMBERS, 128)
    out = update(owner_row, owner_col, cells, obs, obs_x, obs_y, obs_level, obs_value, obs_noise, obs_var)
    return out.reshape(ensemble.shape)


def solution(mesh):
    in_specs = (P(None, None, "gx", "gy"), P(), P(), P(), P(), P(), P(), P(), P())
    out_specs = P(None, None, "gx", "gy")
    return jax.shard_map(shards, mesh=mesh, in_specs=in_specs, out_specs=out_specs, check_vma=False)
```

time: 78.4 us -> 83.4 us (1.064)
  the two profiles are of different devices: /device:TPU:7 before, /device:TPU:1 now
where the time goes in v2:
time: 83.4 us; the launch traced here: 83 us
  Pallas kernels  83 us (100%)
    pallas_call x1, Pallas kernels, update(): pl.pallas_call(update_kernel, out_shape=jax.ShapeDtypeStruct(state.shape,...  41.6 us
    pallas_call x1, Pallas kernels, spread(): pl.pallas_call(spread_kernel, out_shape=jax.ShapeDtypeStruct((2, 16, 40,...  39.8 us

profile of v2, /device:TPU:1, one launch (start us, length us, event | category | flops | bytes accessed | tf_op | source)
XLA Modules:
  0.0 83.0 jit_solution(9919956524270883385)
XLA Ops:
  0.0 1.7 %shard_map.91 = f32[2,8,80,128]{3,2,1,0:T(8,128)} custom-call(s32[2]{0:T(128)} %row_in.3, s32[2]{0:T(128)} %col_in.3, f32[80,32,128]{2,1,0:T(8,128)} %bitcast.4, s32[2,1024]{1,0:T(2,128)} %ox_in.3, s32[2,1024]{1,0:T(2,128)} %oy_in.3, s32[2,1024]{1,0:T(2,128)} %ol_in.3), custom_call_target="tpu_custom_call" | custom-call | tf_op jit(solution)/shard_map/pallas_call | solution.py:308
  1.7 39.8 %shard_map.92 = f32[2,16,40,128]{3,2,1,0:T(8,128)} custom-call(f32[2,16,40,128]{3,2,1,0:T(8,128)} %bitcast.7), custom_call_target="tpu_custom_call" | custom-call | tf_op jit(solution)/shard_map/pallas_call | solution.py:492
  41.4 41.6 %shard_map.93 = f32[80,32,128]{2,1,0:T(8,128)} custom-call(s32[2]{0:T(128)} %row_in.3, s32[2]{0:T(128)} %col_in.3, f32[80,32,128]{2,1,0:T(8,128)} %bitcast.5, f32[2,8,80,128]{3,2,1,0:T(8,128)} %bitcast.6, s32[2,1024]{1,0:T(2,128)} %ox_in.3, s32[2,1024]{1,0:T(2,128)} %oy_in.3, s32[2,1024]{1,0:T(2,128)} %ol_in.3, f32[2,1024]{1,0:T(2,128)} %value_in.1, ...), custom_call_target="tpu_custom_call" | custom-call | tf_op jit(solution)/shard_map/pallas_call | solution.py:329

commit v3 on v2

--- a/solution.py
+++ b/solution.py
@@ -104,8 +104,8 @@
 
 
 def update_kernel(row_in, col_in, state, obs, ox_in, oy_in, ol_in, value_in, noise_in, var_in, out,
-                  row, col, ox, oy, ol, value, var, cells, hx, noises, both, scaled, cast, weights, near_y, col_x, col_y, col_f, taper, keep, gain_hi, gain_lo,
-                  sem_in, sem_obs, sem_out):
+                  row, col, ox, oy, ol, value, var, cells, hx, noises, both, scaled, cast, weights, near_y, col_x, col_y, col_f, taper, keep, gain_hi, gain_lo, passed,
+                  sem_in, sem_obs, sem_out, sem_pass):
     gx = lax.axis_index("gx")
     gy = lax.axis_index("gy")
     small = [(row_in, row), (col_in, col), (ox_in, ox), (oy_in, oy), (ol_in, ol), (value_in, value), (var_in, var)]
@@ -122,7 +122,9 @@
     near = [close(b, gx, gy) for b in range(2)]
     linked = jnp.logical_and(near[1], close(0, row[1], col[1]))
     any_near = jnp.logical_or(near[0], near[1])
-    whole = pltpu.make_async_copy(state, out, sem_out)
+    passing = [pl.ds(20 * i, 20) for i in range(4)]
+    passing_in = [pltpu.make_async_copy(state.at[p], passed.at[p], sem_pass.at[i]) for i, p in enumerate(passing)]
+    passing_out = [pltpu.make_async_copy(passed.at[p], out.at[p], sem_pass.at[i]) for i, p in enumerate(passing)]
     all_in = pltpu.make_async_copy(cells, cells, sem_in)
     all_out = pltpu.make_async_copy(cells, cells, sem_out)
 
@@ -146,8 +148,13 @@
 
     @pl.when(jnp.logical_not(any_near))
     def _():
-        whole.start()
-        whole.wait()
+        for copy in passing_in:
+            copy.start()
+        for one, two in zip(passing_in, passing_out):
+            one.wait()
+            two.start()
+        for copy in passing_out:
+            copy.wait()
 
     def prepare(b):
         lane = lax.broadcasted_iota(jnp.int32, (1, 128), 1)
@@ -354,9 +361,11 @@
             S((2, MEMBERS, MEMBERS), F32),
             S((2, 1024, 256), BF16),
             S((2, 1024, 256), BF16),
+            S((MEMBERS, 32, 128), F32),
             pltpu.SemaphoreType.DMA,
             pltpu.SemaphoreType.DMA((9,)),
             pltpu.SemaphoreType.DMA,
+            pltpu.SemaphoreType.DMA((4,)),
         ],
         compiler_params=pltpu.CompilerParams(vmem_limit_bytes=60 * 2**20),
     )(row, col, state, obs, ox, oy, ol, value, noise, var)

time: 83.4 us -> 56.6 us (0.68)
  Pallas kernels: 83 us -> 56.2 us
    pallas_call x1, Pallas kernels: 41.6 us -> 17 us  [update(): pl.pallas_call(update_kernel, out_shape=jax.ShapeDtypeStruct(state.shape,...]
    pallas_call x1, Pallas kernels: 39.8 us -> 37.5 us  [spread(): pl.pallas_call(spread_kernel, out_shape=jax.ShapeDtypeStruct((2, 16, 40,...]
where the time goes in v3:
time: 56.6 us; the launch traced here: 56.3 us
  Pallas kernels  56.2 us (99%)
    pallas_call x1, Pallas kernels, spread(): pl.pallas_call(spread_kernel, out_shape=jax.ShapeDtypeStruct((2, 16, 40,...  37.5 us
    pallas_call x1, Pallas kernels, update(): pl.pallas_call(update_kernel, out_shape=jax.ShapeDtypeStruct(state.shape,...  17 us
    pallas_call x1, Pallas kernels, pick(): pl.pallas_call(pick_kernel, out_shape=jax.ShapeDtypeStruct((2, 8, MEMBERS...  1.66 us

profile of v3, /device:TPU:1, one launch (start us, length us, event | category | flops | bytes accessed | tf_op | source)
XLA Modules:
  0.0 56.3 jit_solution(11925229357673609610)
XLA Ops:
  0.0 1.7 %shard_map.91 = f32[2,8,80,128]{3,2,1,0:T(8,128)} custom-call(s32[2]{0:T(128)} %row_in.3, s32[2]{0:T(128)} %col_in.3, f32[80,32,128]{2,1,0:T(8,128)} %bitcast.4, s32[2,1024]{1,0:T(2,128)} %ox_in.3, s32[2,1024]{1,0:T(2,128)} %oy_in.3, s32[2,1024]{1,0:T(2,128)} %ol_in.3), custom_call_target="tpu_custom_call" | custom-call | tf_op jit(solution)/shard_map/pallas_call | solution.py:315
  1.7 37.5 %shard_map.92 = f32[2,16,40,128]{3,2,1,0:T(8,128)} custom-call(f32[2,16,40,128]{3,2,1,0:T(8,128)} %bitcast.7), custom_call_target="tpu_custom_call" | custom-call | tf_op jit(solution)/shard_map/pallas_call | solution.py:501
  39.2 17.0 %shard_map.93 = f32[80,32,128]{2,1,0:T(8,128)} custom-call(s32[2]{0:T(128)} %row_in.3, s32[2]{0:T(128)} %col_in.3, f32[80,32,128]{2,1,0:T(8,128)} %bitcast.5, f32[2,8,80,128]{3,2,1,0:T(8,128)} %bitcast.6, s32[2,1024]{1,0:T(2,128)} %ox_in.3, s32[2,1024]{1,0:T(2,128)} %oy_in.3, s32[2,1024]{1,0:T(2,128)} %ol_in.3, f32[2,1024]{1,0:T(2,128)} %value_in.1, ...), custom_call_target="tpu_custom_call" | custom-call | tf_op jit(solution)/shard_map/pallas_call | solution.py:336

commit v4 on v2

--- a/solution.py
+++ b/solution.py
@@ -22,51 +22,6 @@
 
 def dot(a, b, dims=NN, precision=None):
     return lax.dot_general(a, b, dims, precision=precision, preferred_element_type=F32)
-
-
-def pick_kernel(row_in, col_in, state, ox_in, oy_in, ol_in, out, row, col, ox, oy, ol, cells, sem, sem_cells):
-    gx = lax.axis_index("gx")
-    gy = lax.axis_index("gy")
-    small = [(row_in, row), (col_in, col), (ox_in, ox), (oy_in, oy), (ol_in, ol)]
-    small = [pltpu.make_async_copy(src, dst, sem.at[i]) for i, (src, dst) in enumerate(small)]
-    for copy in small:
-        copy.start()
-    small[0].wait()
-    small[1].wait()
-    owned = [jnp.logical_and(row[b] == gx, col[b] == gy) for b in range(2)]
-
-    @pl.when(jnp.logical_or(owned[0], owned[1]))
-    def _():
-        @pl.loop(0, 32)
-        def _(r):
-            pltpu.make_async_copy(state.at[:, r], cells.at[r], sem_cells).start()
-
-    for copy in small[2:]:
-        copy.wait()
-
-    @pl.when(jnp.logical_or(owned[0], owned[1]))
-    def _():
-        pltpu.make_async_copy(cells, cells, sem_cells).wait()
-
-    for b in range(2):
-
-        @pl.when(owned[b])
-        def _():
-            @pl.loop(0, 8)
-            def _(c):
-                cols = pl.ds(pl.multiple_of(c * 128, 128), 128)
-                want = jnp.broadcast_to(ol[b : b + 1, cols] * 8 + ox[b : b + 1, cols], (8, 128))
-                at = jnp.broadcast_to(oy[b : b + 1, cols], (8, 128))
-                for k in range(0, MEMBERS, 8):
-                    got = jnp.zeros((8, 128), F32)
-                    for r in range(32):
-                        moved = jnp.take_along_axis(cells[r, k : k + 8], at, axis=1, mode="promise_in_bounds")
-                        got = jnp.where(want == r, moved, got)
-                    out[b, c, k : k + 8] = got
-
-        @pl.when(jnp.logical_not(owned[b]))
-        def _():
-            out[b] = jnp.zeros((8, MEMBERS, 128), F32)
 
 
 def inverse_of(a, keep):
@@ -103,16 +58,27 @@
     return keep[0]
 
 
-def update_kernel(row_in, col_in, state, obs, ox_in, oy_in, ol_in, value_in, noise_in, var_in, out,
-                  row, col, ox, oy, ol, value, var, cells, hx, noises, both, scaled, cast, weights, near_y, col_x, col_y, col_f, taper, keep, gain_hi, gain_lo,
-                  sem_in, sem_obs, sem_out):
+def update_kernel(row_in, col_in, state, obs_in, ox_in, oy_in, ol_in, value_in, noise_in, var_in, out,
+                  row, col, ox, oy, ol, value, var, obs, noises, cells, hx, both, scaled, cast, weights, near_y, col_x, col_y, col_f, taper, keep, gain_hi, gain_lo,
+                  sem_in, sem_small, sem_out):
     gx = lax.axis_index("gx")
     gy = lax.axis_index("gy")
     small = [(row_in, row), (col_in, col), (ox_in, ox), (oy_in, oy), (ol_in, ol), (value_in, value), (var_in, var)]
-    small += [(obs, hx), (noise_in, noises)]
-    small = [pltpu.make_async_copy(src, dst, sem_obs.at[i]) for i, (src, dst) in enumerate(small)]
-    for copy in small[:2]:
+    small += [(obs_in, obs), (noise_in, noises)]
+    small = [pltpu.make_async_copy(src, dst, sem_small.at[i]) for i, (src, dst) in enumerate(small)]
+    for copy in small:
         copy.start()
+
+    def fetch(r):
+        return pltpu.make_async_copy(state.at[:, r], cells.at[r], sem_in)
+
+    def store(r):
+        return pltpu.make_async_copy(cells.at[r], out.at[:, r], sem_out)
+
+    @pl.loop(0, 32)
+    def _(r):
+        fetch(r).start()
+
     for copy in small[:2]:
         copy.wait()
 
@@ -122,41 +88,27 @@
     near = [close(b, gx, gy) for b in range(2)]
     linked = jnp.logical_and(near[1], close(0, row[1], col[1]))
     any_near = jnp.logical_or(near[0], near[1])
-    whole = pltpu.make_async_copy(state, out, sem_out)
     all_in = pltpu.make_async_copy(cells, cells, sem_in)
     all_out = pltpu.make_async_copy(cells, cells, sem_out)
 
-    def fetch(r):
-        return pltpu.make_async_copy(state.at[:, r], cells.at[r], sem_in)
-
-    def store(r):
-        return pltpu.make_async_copy(cells.at[r], out.at[:, r], sem_out)
-
-    @pl.when(any_near)
-    def _():
-        for copy in small[2:]:
-            copy.start()
-
-        @pl.loop(0, 32)
-        def _(r):
-            fetch(r).start()
-
-        for copy in small[2:]:
-            copy.wait()
-
-    @pl.when(jnp.logical_not(any_near))
-    def _():
-        whole.start()
-        whole.wait()
-
-    def prepare(b):
+    for copy in small[2:]:
+        copy.wait()
+
+    @pl.when(linked)
+    def _():
+        hx[...] = obs[1]
+
+    def members_of(ref, c):
+        return jnp.concatenate([ref[2 * c + j] for j in range(2)], axis=0)
+
+    def prepare(b, source):
         lane = lax.broadcasted_iota(jnp.int32, (1, 128), 1)
         mesh_y = (gy * 128 + lane - col[b] * 128).astype(F32) * (1.0 / LOC)
 
         @pl.loop(0, 8)
         def _(c):
             cols = pl.ds(pl.multiple_of(c * 128, 128), 128)
-            h = hx[b, c]
+            h = members_of(source, c)
             inv = 1.0 / var[b : b + 1, cols]
             o = h - jnp.sum(h, axis=0, keepdims=True) * (1.0 / MEMBERS)
             d = value[b : b + 1, cols] + noises[b, :, cols] - h
@@ -270,16 +222,22 @@
                     f = jnp.where(lev == level, col_f[level, span, :], f)
                 return t * t * f
 
-            h = hx[1, c]
-            hx[1, c] = h + gain(h, 4, taper_at)
+            h = members_of(hx, c)
+            h = h + gain(h, 4, taper_at)
+            for j in range(2):
+                hx[2 * c + j] = h[40 * j : 40 * j + 40]
 
     @pl.when(jnp.logical_or(near[0], linked))
     def _():
-        prepare(0)
-
-    @pl.when(any_near)
-    def _():
-        all_in.wait()
+        prepare(0, obs.at[0])
+
+    all_in.wait()
+
+    @pl.when(jnp.logical_not(any_near))
+    def _():
+        @pl.loop(0, 32)
+        def _(r):
+            store(r).start()
 
     @pl.when(near[0])
     def _():
@@ -291,37 +249,19 @@
 
     @pl.when(near[1])
     def _():
-        prepare(1)
+        @pl.when(jnp.logical_not(linked))
+        def _():
+            hx[...] = obs[1]
+
+        prepare(1, hx)
         move_state(1, True)
 
-    @pl.when(any_near)
-    def _():
-        all_out.wait()
+    all_out.wait()
 
 
 VMEM = pl.BlockSpec(memory_space=pltpu.VMEM)
 SMEM = pl.BlockSpec(memory_space=pltpu.SMEM)
 ANY = pl.BlockSpec(memory_space=pl.ANY)
-
-
-def pick(row, col, state, ox, oy, ol):
-    return pl.pallas_call(
-        pick_kernel,
-        out_shape=jax.ShapeDtypeStruct((2, 8, MEMBERS, 128), F32),
-        in_specs=[ANY] * 6,
-        out_specs=VMEM,
-        scratch_shapes=[
-            pltpu.SMEM((2,), jnp.int32),
-            pltpu.SMEM((2,), jnp.int32),
-            pltpu.VMEM((2, 1024), jnp.int32),
-            pltpu.VMEM((2, 1024), jnp.int32),
-            pltpu.VMEM((2, 1024), jnp.int32),
-            pltpu.VMEM((32, MEMBERS, 128), F32),
-            pltpu.SemaphoreType.DMA((5,)),
-            pltpu.SemaphoreType.DMA,
-        ],
-        compiler_params=pltpu.CompilerParams(vmem_limit_bytes=60 * 2**20),
-    )(row, col, state, ox, oy, ol)
 
 
 def update(row, col, state, obs, ox, oy, ol, value, noise, var):
@@ -339,9 +279,10 @@
             S((2, 1024), jnp.int32),
             S((2, 1024), F32),
             S((2, 1024), F32),
+            S((2, 16, 40, 128), F32),
+            S((2, MEMBERS, 1024), F32),
             S((32, MEMBERS, 128), F32),
-            S((2, 8, MEMBERS, 128), F32),
-            S((2, MEMBERS, 1024), F32),
+            S((16, 40, 128), F32),
             S((160, 1024), F32),
             S((MEMBERS, 1024), F32),
             S((5, 1024, 256), BF16),
@@ -364,8 +305,13 @@
 
 MESH = pl.DeviceIdType.MESH
 
-def spread_kernel(piece, out, pair_buf, acc, ring_buf, z_src, z_buf,
-                  s0s, s0r, s1s, s1r, s2s, s2r, s3s, s3r, s4s, s4r):
+
+FAR = sorted(((dx, dy) for dx in range(4) for dy in range(4) if dx or dy), key=lambda o: -sum(min(d, 4 - d) for d in o))
+
+
+def spread_kernel(row_in, col_in, state, ox_in, oy_in, ol_in, out,
+                  row, col, ox, oy, ol, cells, piece, pair_buf, acc, ring_buf, z_src, z_buf,
+                  sem, sem_cells, s0s, s0r, s1s, s1r, s2s, s2r, s3s, s3r, s4s, s4r):
     gx = lax.axis_index("gx")
     gy = lax.axis_index("gy")
     yy = gx // 4
@@ -384,6 +330,17 @@
         return (yy * 4 + t // 2, (t % 2) * 8 + xx * 2 + core)
 
     mate = (gx, zl * 8 + xx * 2 + other)
+    ahead = [((yy + dy) % 4) * 4 + (xx + dx) % 4 for dx, dy in FAR]
+    behind = [((yy + 4 - dy) % 4) * 4 + (xx + 4 - dx) % 4 for dx, dy in reversed(FAR)]
+
+    small = [(row_in, row), (col_in, col), (ox_in, ox), (oy_in, oy), (ol_in, ol)]
+    small = [pltpu.make_async_copy(src, dst, sem.at[i]) for i, (src, dst) in enumerate(small)]
+    for copy in small:
+        copy.start()
+
+    @pl.loop(0, 32)
+    def _(r):
+        pltpu.make_async_copy(state.at[:, r], cells.at[r], sem_cells).start()
 
     barrier = pltpu.get_barrier_semaphore()
 
@@ -396,84 +353,95 @@
         pl.semaphore_signal(barrier, inc=1, device_id=dev_z((z + d) % 8), device_id_type=MESH)
 
     pl.semaphore_signal(barrier, inc=1, device_id=mate, device_id_type=MESH)
+
+    for copy in small:
+        copy.wait()
+    pltpu.make_async_copy(cells, cells, sem_cells).wait()
+
+    def gather(b, g):
+        cols = pl.ds(pl.multiple_of(g * 128, 128), 128)
+        mine = jnp.logical_and(row[b] == gx, col[b] == gy).astype(F32)
+        want = ol[:, cols] * 8 + ox[:, cols]
+        want = jnp.broadcast_to(jnp.where(b == 0, want[0:1], want[1:2]), (8, 128))
+        at = oy[:, cols]
+        at = jnp.broadcast_to(jnp.where(b == 0, at[0:1], at[1:2]), (8, 128))
+        for k in range(0, MEMBERS, 8):
+            got = jnp.zeros((8, 128), F32)
+            for r in range(32):
+                moved = jnp.take_along_axis(cells[r, k : k + 8], at, axis=1, mode="promise_in_bounds")
+                got = jnp.where(want == r, moved, got)
+            piece[b, 2 * g + k // 40, k % 40 : k % 40 + 8] = got * mine
+
+    def remote(src, dst, send, recv, to):
+        return pltpu.make_async_remote_copy(
+            src_ref=src, dst_ref=dst, send_sem=send, recv_sem=recv, device_id=to, device_id_type=MESH)
+
+    def c0(g):
+        two = pl.ds(2 * g, 2)
+        return remote(piece.at[other, two], pair_buf.at[two], s0s.at[g], s0r.at[g], mate)
+
+    def c1(t, slot):
+        return remote(acc.at[t], ring_buf.at[slot], s1s.at[t], s1r.at[slot], dev_xy(t))
+
+    def c2(t, slot):
+        return remote(z_src, z_buf.at[slot], s2s.at[t], s2r.at[slot], dev_z(t))
+
+    def c3(t, slot):
+        return remote(out.at[core, slot], out.at[core, slot], s3s.at[t], s3r.at[slot], dev_xy(t))
+
+    def c4(b, slot):
+        return remote(out.at[b, slot], out.at[b, slot], s4s.at[slot], s4r.at[slot], mate)
+
     pl.semaphore_wait(barrier, 23)
 
-    def c0(t):
-        return pltpu.make_async_remote_copy(
-            src_ref=piece.at[other, t], dst_ref=pair_buf.at[t], send_sem=s0s.at[t], recv_sem=s0r.at[t],
-            device_id=mate, device_id_type=MESH)
-
-    def c1(t, slot):
-        return pltpu.make_async_remote_copy(
-            src_ref=acc.at[t], dst_ref=ring_buf.at[slot], send_sem=s1s.at[t], recv_sem=s1r.at[slot],
-            device_id=dev_xy(t), device_id_type=MESH)
-
-    def c2(t, slot):
-        return pltpu.make_async_remote_copy(
-            src_ref=z_src, dst_ref=z_buf.at[slot], send_sem=s2s.at[t], recv_sem=s2r.at[slot],
-            device_id=dev_z(t), device_id_type=MESH)
-
-    def c3(t, slot):
-        return pltpu.make_async_remote_copy(
-            src_ref=out.at[core, slot], dst_ref=out.at[core, slot], send_sem=s3s.at[t], recv_sem=s3r.at[slot],
-            device_id=dev_xy(t), device_id_type=MESH)
-
-    def c4(w, slot):
-        return pltpu.make_async_remote_copy(
-            src_ref=out.at[w, slot], dst_ref=out.at[w, slot], send_sem=s4s.at[slot], recv_sem=s4r.at[slot],
-            device_id=mate, device_id_type=MESH)
-
-    @pl.loop(1, 17)
-    def _(d):
-        c0((q + d) % 16).start()
-
-    @pl.loop(1, 16)
-    def _(d):
-        t = (q + d) % 16
-        c0(t).wait_recv()
-        acc[t] = piece[core, t] + pair_buf[t]
-        c1(t, q).start()
-
-    c0(q).wait_recv()
-    z_src[...] = piece[core, q] + pair_buf[q]
-
-    @pl.loop(1, 16)
-    def _(d):
-        t = (q + 16 - d) % 16
+    @pl.loop(0, 8)
+    def _(i):
+        g = (q // 2 + 1 + i) % 8
+        gather(other, g)
+        c0(g).start()
+
+    @pl.loop(0, 8)
+    def _(i):
+        g = (q // 2 + 1 + i) % 8
+        gather(core, g)
+        c0(g).wait_recv()
+        for j in range(2):
+            t = 2 * g + j
+            acc[t] = piece[core, t] + pair_buf[t]
+
+            @pl.when(t != q)
+            def _():
+                c1(t, q).start()
+
+    total = acc[q]
+    for t in behind:
         c1(t, t).wait_recv()
-        z_src[...] += ring_buf[t]
-
-    @pl.loop(1, 8)
-    def _(d):
+        total = total + ring_buf[t]
+    z_src[...] = total
+    for d in (4, 3, 5, 2, 6, 1, 7):
         c2((z + d) % 8, z).start()
-
-    out[core, q] = z_src[...]
-
-    @pl.loop(1, 8)
-    def _(d):
+    for d in (1, 7, 2, 6, 3, 5, 4):
         t = (z + 8 - d) % 8
         c2(t, t).wait_recv()
-        out[core, q] += z_buf[t]
-
-    @pl.loop(1, 16)
-    def _(d):
-        c3((q + d) % 16, q).start()
-
+        total = total + z_buf[t]
+    out[core, q] = total
+    for t in ahead:
+        c3(t, q).start()
     c4(core, q).start()
-
-    @pl.loop(1, 16)
-    def _(d):
-        t = (q + 16 - d) % 16
+    for t in behind:
         c3(t, t).wait_recv()
         c4(core, t).start()
 
     @pl.loop(0, 16)
-    def _(d):
-        c4(other, (q + 16 - d) % 16).wait_recv()
+    def _(t):
+        c4(other, t).wait_recv()
+
+    @pl.loop(0, 8)
+    def _(g):
+        c0(g).wait_send()
 
     @pl.loop(0, 16)
     def _(t):
-        c0(t).wait_send()
         c4(core, t).wait_send()
 
     @pl.loop(1, 16)
@@ -487,29 +455,38 @@
         c2((z + d) % 8, z).wait_send()
 
 
-def spread(piece):
+def spread(row, col, state, ox, oy, ol):
     D = pltpu.SemaphoreType.DMA
+    S = pltpu.VMEM
     return pl.pallas_call(
         spread_kernel,
-        out_shape=jax.ShapeDtypeStruct((2, 16, 40, 128), jnp.float32),
-        in_specs=[pl.BlockSpec(memory_space=pltpu.VMEM)],
-        out_specs=pl.BlockSpec(memory_space=pltpu.VMEM),
+        out_shape=jax.ShapeDtypeStruct((2, 16, 40, 128), F32),
+        in_specs=[ANY] * 6,
+        out_specs=VMEM,
         scratch_shapes=[
-            pltpu.VMEM((16, 40, 128), jnp.float32),
-            pltpu.VMEM((16, 40, 128), jnp.float32),
-            pltpu.VMEM((16, 40, 128), jnp.float32),
-            pltpu.VMEM((40, 128), jnp.float32),
-            pltpu.VMEM((8, 40, 128), jnp.float32),
-            D((16,)), D((16,)), D((16,)), D((16,)), D((8,)), D((8,)), D((16,)), D((16,)), D((16,)), D((16,)),
+            pltpu.SMEM((2,), jnp.int32),
+            pltpu.SMEM((2,), jnp.int32),
+            S((2, 1024), jnp.int32),
+            S((2, 1024), jnp.int32),
+            S((2, 1024), jnp.int32),
+            S((32, MEMBERS, 128), F32),
+            S((2, 16, 40, 128), F32),
+            S((16, 40, 128), F32),
+            S((16, 40, 128), F32),
+            S((16, 40, 128), F32),
+            S((40, 128), F32),
+            S((8, 40, 128), F32),
+            D((5,)), D,
+            D((8,)), D((8,)), D((16,)), D((16,)), D((8,)), D((8,)), D((16,)), D((16,)), D((16,)), D((16,)),
         ],
-        compiler_params=pltpu.CompilerParams(collective_id=0, has_side_effects=True),
-    )(piece)
+        compiler_params=pltpu.CompilerParams(
+            collective_id=0, has_side_effects=True, vmem_limit_bytes=60 * 2**20),
+    )(row, col, state, ox, oy, ol)
 
 
 def shards(ensemble, obs_x, obs_y, obs_level, owner_row, owner_col, obs_value, obs_noise, obs_var):
     cells = ensemble.reshape(MEMBERS, 32, 128)
-    piece = pick(owner_row, owner_col, cells, obs_x, obs_y, obs_level)
-    obs = spread(piece.reshape(2, 16, 40, 128)).reshape(2, 8, MEMBERS, 128)
+    obs = spread(owner_row, owner_col, cells, obs_x, obs_y, obs_level)
     out = update(owner_row, owner_col, cells, obs, obs_x, obs_y, obs_level, obs_value, obs_noise, obs_var)
     return out.reshape(ensemble.shape)
 

time: 83.4 us -> 51.8 us (0.62)
  the two profiles are of different devices: /device:TPU:1 before, /device:TPU:9 now
where the time goes in v4:
time: 51.8 us; the launch traced here: 51.5 us
  Pallas kernels  51.5 us (99%)
    pallas_call x1, Pallas kernels, spread(): pl.pallas_call(spread_kernel, out_shape=jax.ShapeDtypeStruct((2, 16, 40,...  35.2 us
    pallas_call x1, Pallas kernels, update(): pl.pallas_call(update_kernel, out_shape=jax.ShapeDtypeStruct(state.shape,...  16.3 us

profile of v4, /device:TPU:9, one launch (start us, length us, event | category | flops | bytes accessed | tf_op | source)
XLA Modules:
  0.0 51.5 jit_solution(14665398425243124109)
XLA Ops:
  0.0 35.2 %shard_map.91.obs_in = f32[2,16,40,128]{3,2,1,0:T(8,128)} custom-call(s32[2]{0:T(128)} %row_in.3, s32[2]{0:T(128)} %col_in.3, f32[80,32,128]{2,1,0:T(8,128)} %bitcast.2, s32[2,1024]{1,0:T(2,128)} %ox_in.3, s32[2,1024]{1,0:T(2,128)} %oy_in.3, s32[2,1024]{1,0:T(2,128)} %ol_in.3), custom_call_target="tpu_custom_call" | custom-call | tf_op jit(solution)/shard_map/pallas_call | solution.py:461
  35.2 16.3 %shard_map.92 = f32[80,32,128]{2,1,0:T(8,128)} custom-call(s32[2]{0:T(128)} %row_in.3, s32[2]{0:T(128)} %col_in.3, f32[80,32,128]{2,1,0:T(8,128)} %bitcast.3, f32[2,16,40,128]{3,2,1,0:T(8,128)} %shard_map.91.obs_in, s32[2,1024]{1,0:T(2,128)} %ox_in.3, s32[2,1024]{1,0:T(2,128)} %oy_in.3, s32[2,1024]{1,0:T(2,128)} %ol_in.3, f32[2,1024]{1,0:T(2,128)} %value_in.1, ...), custom_call_target="tpu_custom_call" | custom-call | tf_op jit(solution)/shard_map/pallas_call | solution.py:269

commit v5 on v4

--- a/solution.py
+++ b/solution.py
@@ -164,8 +164,8 @@
     def gain(values, level, taper_at, slot=0):
         right = spread_of(values)
         wide = values.shape[1]
-        for part in range(4):
-            span = slice(part * 256, part * 256 + 256)
+        for part in range(2):
+            span = slice(part * 512, part * 512 + 512)
             cross = dot(cast[level, span, :], right)
             hi, lo = split(cross * taper_at(span))
             gain_hi[slot, span, 0:wide] = hi
@@ -177,22 +177,24 @@
     def move_state(b, last):
         @pl.loop(0, 4)
         def _(pair):
-            for half in range(2):
-                x = (gx * 8 + pair * 2 + half - row[b] * 8).astype(F32) * (1.0 / LOC)
-
-                @pl.loop(0, 8)
-                def _(c):
-                    cols = pl.ds(pl.multiple_of(c * 128, 128), 128)
-                    dx = x - col_x[cols, :]
-                    t = jnp.maximum(near_y[cols, :] - dx * dx, 0.0)
-                    taper[cols, half * 128 : half * 128 + 128] = t * t
+            x = [(gx * 8 + pair * 2 + half - row[b] * 8).astype(F32) * (1.0 / LOC) for half in range(2)]
+
+            def taper_at(span):
+                parts = []
+                for half in range(2):
+                    dx = x[half] - col_x[span, :]
+                    t = jnp.maximum(near_y[span, :] - dx * dx, 0.0)
+                    parts.append(t * t)
+                t = jnp.concatenate(parts, axis=1)
+                taper[span, :] = t
+                return t
 
             before = []
             for level in range(4):
                 before.append([cells[level * 8 + pair * 2 + half] for half in range(2)])
             after = []
             for level in range(4):
-                change = gain(jnp.concatenate(before[level], axis=1), level, lambda span: taper[span, :], level % 2)
+                change = gain(jnp.concatenate(before[level], axis=1), level, (lambda span: taper[span, :]) if level else taper_at, level % 2)
                 after.append([before[level][half] + change[:, half * 128 : half * 128 + 128] for half in range(2)])
             for level in range(4):
                 for half in range(2):
@@ -206,26 +208,31 @@
                         pl.when(last)(store(r).start)
 
     def move_obs():
-        @pl.loop(0, 8)
+        @pl.loop(0, 4)
         def _(c):
-            cols = pl.ds(pl.multiple_of(c * 128, 128), 128)
+            cols = pl.ds(pl.multiple_of(c * 256, 256), 256)
             x = (ox[1:2, cols] + (row[1] - row[0]) * 8).astype(F32) * (1.0 / LOC)
             y = (oy[1:2, cols] + (col[1] - col[0]) * 128).astype(F32) * (1.0 / LOC)
             lev = ol[1:2, cols]
+            at = [lev == level for level in range(3)]
 
             def taper_at(span):
-                dx = x - col_x[span, :]
-                dy = y - col_y[span, :]
-                t = jnp.maximum(1.0 - (dx * dx + dy * dy), 0.0)
-                f = col_f[3, span, :]
-                for level in range(3):
-                    f = jnp.where(lev == level, col_f[level, span, :], f)
-                return t * t * f
-
-            h = members_of(hx, c)
+                parts = []
+                for half in range(2):
+                    here = slice(half * 128, half * 128 + 128)
+                    dx = x[:, here] - col_x[span, :]
+                    dy = y[:, here] - col_y[span, :]
+                    t = jnp.maximum(1.0 - (dx * dx + dy * dy), 0.0)
+                    f = col_f[3, span, :]
+                    for level in range(3):
+                        f = jnp.where(at[level][:, here], col_f[level, span, :], f)
+                    parts.append(t * t * f)
+                return jnp.concatenate(parts, axis=1)
+
+            h = jnp.concatenate([members_of(hx, 2 * c + half) for half in range(2)], axis=1)
             h = h + gain(h, 4, taper_at)
-            for j in range(2):
-                hx[2 * c + j] = h[40 * j : 40 * j + 40]
+            for j in range(4):
+                hx[4 * c + j] = h[40 * (j % 2) : 40 * (j % 2) + 40, 128 * (j // 2) : 128 * (j // 2) + 128]
 
     @pl.when(jnp.logical_or(near[0], linked))
     def _():
@@ -310,8 +317,8 @@
 
 
 def spread_kernel(row_in, col_in, state, ox_in, oy_in, ol_in, out,
-                  row, col, ox, oy, ol, cells, piece, pair_buf, acc, ring_buf, z_src, z_buf,
-                  sem, sem_cells, s0s, s0r, s1s, s1r, s2s, s2r, s3s, s3r, s4s, s4r):
+                  row, col, ox, oy, ol, cells, piece, pair_buf, acc, ring_buf, z_src, z_buf, full,
+                  sem, sem_cells, sem_out, s0s, s0r, s1s, s1r, s2s, s2r, s3s, s3r, s4s, s4r):
     gx = lax.axis_index("gx")
     gy = lax.axis_index("gy")
     yy = gx // 4
@@ -387,22 +394,30 @@
         return remote(z_src, z_buf.at[slot], s2s.at[t], s2r.at[slot], dev_z(t))
 
     def c3(t, slot):
-        return remote(out.at[core, slot], out.at[core, slot], s3s.at[t], s3r.at[slot], dev_xy(t))
+        return remote(full.at[slot], full.at[slot], s3s.at[t], s3r.at[slot], dev_xy(t))
 
     def c4(b, slot):
-        return remote(out.at[b, slot], out.at[b, slot], s4s.at[slot], s4r.at[slot], mate)
+        return remote(full.at[slot], out.at[b, slot], s4s.at[slot], s4r.at[slot], mate)
+
+    def keep(slot):
+        return pltpu.make_async_copy(full.at[slot], out.at[core, slot], sem_out.at[slot])
+
+    def nth_group(i):
+        step = i // 2
+        dy = jnp.where(step == 0, 2, jnp.where(step == 1, 1, jnp.where(step == 2, 3, 0)))
+        return ((yy + dy) % 4) * 2 + (xx // 2 + 1 + i) % 2
 
     pl.semaphore_wait(barrier, 23)
 
     @pl.loop(0, 8)
     def _(i):
-        g = (q // 2 + 1 + i) % 8
+        g = nth_group(i)
         gather(other, g)
         c0(g).start()
 
     @pl.loop(0, 8)
     def _(i):
-        g = (q // 2 + 1 + i) % 8
+        g = nth_group(i)
         gather(core, g)
         c0(g).wait_recv()
         for j in range(2):
@@ -424,13 +439,15 @@
         t = (z + 8 - d) % 8
         c2(t, t).wait_recv()
         total = total + z_buf[t]
-    out[core, q] = total
+    full[q] = total
     for t in ahead:
         c3(t, q).start()
     c4(core, q).start()
+    keep(q).start()
     for t in behind:
         c3(t, t).wait_recv()
         c4(core, t).start()
+        keep(t).start()
 
     @pl.loop(0, 16)
     def _(t):
@@ -443,6 +460,7 @@
     @pl.loop(0, 16)
     def _(t):
         c4(core, t).wait_send()
+        keep(t).wait()
 
     @pl.loop(1, 16)
     def _(d):
@@ -462,7 +480,7 @@
         spread_kernel,
         out_shape=jax.ShapeDtypeStruct((2, 16, 40, 128), F32),
         in_specs=[ANY] * 6,
-        out_specs=VMEM,
+        out_specs=ANY,
         scratch_shapes=[
             pltpu.SMEM((2,), jnp.int32),
             pltpu.SMEM((2,), jnp.int32),
@@ -476,7 +494,8 @@
             S((16, 40, 128), F32),
             S((40, 128), F32),
             S((8, 40, 128), F32),
-            D((5,)), D,
+            S((16, 40, 128), F32),
+            D((5,)), D, D((16,)),
             D((8,)), D((8,)), D((16,)), D((16,)), D((8,)), D((8,)), D((16,)), D((16,)), D((16,)), D((16,)),
         ],
         compiler_params=pltpu.CompilerParams(

time: 51.8 us -> 50.9 us (0.983)
  the two profiles are of different devices: /device:TPU:9 before, /device:TPU:7 now
where the time goes in v5:
time: 50.9 us; the launch traced here: 50.6 us
  Pallas kernels  50.6 us (99%)
    pallas_call x1, Pallas kernels, spread(): pl.pallas_call(spread_kernel, out_shape=jax.ShapeDtypeStruct((2, 16, 40,...  34.4 us
    pallas_call x1, Pallas kernels, update(): pl.pallas_call(update_kernel, out_shape=jax.ShapeDtypeStruct(state.shape,...  16.2 us

profile of v5, /device:TPU:7, one launch (start us, length us, event | category | flops | bytes accessed | tf_op | source)
XLA Modules:
  0.0 50.6 jit_solution(12552261456581074464)
XLA Ops:
  0.0 34.4 %shard_map.91.obs_in = f32[2,16,40,128]{3,2,1,0:T(8,128)} custom-call(s32[2]{0:T(128)} %row_in.3, s32[2]{0:T(128)} %col_in.3, f32[80,32,128]{2,1,0:T(8,128)} %bitcast.2, s32[2,1024]{1,0:T(2,128)} %ox_in.3, s32[2,1024]{1,0:T(2,128)} %oy_in.3, s32[2,1024]{1,0:T(2,128)} %ol_in.3), custom_call_target="tpu_custom_call" | custom-call | tf_op jit(solution)/shard_map/pallas_call | solution.py:479
  34.4 16.2 %shard_map.92 = f32[80,32,128]{2,1,0:T(8,128)} custom-call(s32[2]{0:T(128)} %row_in.3, s32[2]{0:T(128)} %col_in.3, f32[80,32,128]{2,1,0:T(8,128)} %bitcast.3, f32[2,16,40,128]{3,2,1,0:T(8,128)} %shard_map.91.obs_in, s32[2,1024]{1,0:T(2,128)} %ox_in.3, s32[2,1024]{1,0:T(2,128)} %oy_in.3, s32[2,1024]{1,0:T(2,128)} %ol_in.3, f32[2,1024]{1,0:T(2,128)} %value_in.1, ...), custom_call_target="tpu_custom_call" | custom-call | tf_op jit(solution)/shard_map/pallas_call | solution.py:276

commit v6 on v5

--- a/solution.py
+++ b/solution.py
@@ -105,7 +105,7 @@
         lane = lax.broadcasted_iota(jnp.int32, (1, 128), 1)
         mesh_y = (gy * 128 + lane - col[b] * 128).astype(F32) * (1.0 / LOC)
 
-        @pl.loop(0, 8)
+        @pl.loop(0, 8, unroll=4)
         def _(c):
             cols = pl.ds(pl.multiple_of(c * 128, 128), 128)
             h = members_of(source, c)
@@ -114,7 +114,10 @@
             d = value[b : b + 1, cols] + noises[b, :, cols] - h
             both[0:MEMBERS, cols] = o
             both[MEMBERS : 2 * MEMBERS, cols] = d
-            scaled[:, cols] = o * inv
+            for n, part in enumerate((o * inv, d * inv)):
+                hi, lo = split(part)
+                scaled[n * MEMBERS : (n + 1) * MEMBERS, cols] = hi
+                scaled[(n + 2) * MEMBERS : (n + 3) * MEMBERS, cols] = lo
             lev = ol[b : b + 1, cols].astype(F32)
             extra = [ox[b : b + 1, cols].astype(F32) * (1.0 / LOC), oy[b : b + 1, cols].astype(F32) * (1.0 / LOC)]
             for level in range(4):
@@ -141,7 +144,8 @@
                 cast[level, cols, 0:128] = left.astype(BF16)
                 cast[level, cols, 128:256] = jnp.where(lane < 32, hi, right - hi).astype(BF16)
 
-        gram = dot(both[...], scaled[...], NT, HIGH)
+        gram = dot(scaled[...], cast[4])
+        gram = gram[0:160, 0:80] + gram[0:160, 160:240] + gram[160:320, 0:80]
         inner = gram[0:MEMBERS]
         eye = lax.broadcasted_iota(jnp.int32, (MEMBERS, MEMBERS), 0) == lax.broadcasted_iota(
             jnp.int32, (MEMBERS, MEMBERS), 1
@@ -175,7 +179,7 @@
         return total[0:MEMBERS] + total[MEMBERS : 2 * MEMBERS] + rest
 
     def move_state(b, last):
-        @pl.loop(0, 4)
+        @pl.loop(0, 4, unroll=2)
         def _(pair):
             x = [(gx * 8 + pair * 2 + half - row[b] * 8).astype(F32) * (1.0 / LOC) for half in range(2)]
 
@@ -291,7 +295,7 @@
             S((32, MEMBERS, 128), F32),
             S((16, 40, 128), F32),
             S((160, 1024), F32),
-            S((MEMBERS, 1024), F32),
+            S((4 * MEMBERS, 1024), BF16),
             S((5, 1024, 256), BF16),
             S((160, 1024), BF16),
             S((1024, 128), F32),
@@ -407,13 +411,21 @@
         dy = jnp.where(step == 0, 2, jnp.where(step == 1, 1, jnp.where(step == 2, 3, 0)))
         return ((yy + dy) % 4) * 2 + (xx // 2 + 1 + i) % 2
 
-    pl.semaphore_wait(barrier, 23)
-
     @pl.loop(0, 8)
     def _(i):
-        g = nth_group(i)
-        gather(other, g)
-        c0(g).start()
+        gather(other, nth_group(i))
+
+        @pl.when(i == 5)
+        def _():
+            pl.semaphore_wait(barrier, 23)
+
+            @pl.loop(0, 5)
+            def _(e):
+                c0(nth_group(e)).start()
+
+        @pl.when(i >= 5)
+        def _():
+            c0(nth_group(i)).start()
 
     @pl.loop(0, 8)
     def _(i):

time: 50.9 us -> 61.5 us (1.21)
  the two profiles are of different devices: /device:TPU:7 before, /device:TPU:57 now
where the time goes in v6:
time: 61.5 us; the launch traced here: 61.2 us
  Pallas kernels  61 us (99%)
    pallas_call x1, Pallas kernels, spread(): pl.pallas_call(spread_kernel, out_shape=jax.ShapeDtypeStruct((2, 16, 40,...  31.4 us
    pallas_call x1, Pallas kernels, update(): pl.pallas_call(update_kernel, out_shape=jax.ShapeDtypeStruct(state.shape,...  29.7 us

profile of v6, /device:TPU:57, one launch (start us, length us, event | category | flops | bytes accessed | tf_op | source)
XLA Modules:
  0.0 61.2 jit_solution(6436782560948123584)
XLA Ops:
  0.0 31.4 %shard_map.91.obs_in = f32[2,16,40,128]{3,2,1,0:T(8,128)} custom-call(s32[2]{0:T(128)} %row_in.3, s32[2]{0:T(128)} %col_in.3, f32[80,32,128]{2,1,0:T(8,128)} %bitcast.2, s32[2,1024]{1,0:T(2,128)} %ox_in.3, s32[2,1024]{1,0:T(2,128)} %oy_in.3, s32[2,1024]{1,0:T(2,128)} %ol_in.3), custom_call_target="tpu_custom_call" | custom-call | tf_op jit(solution)/shard_map/pallas_call | solution.py:491
  31.4 29.7 %shard_map.92 = f32[80,32,128]{2,1,0:T(8,128)} custom-call(s32[2]{0:T(128)} %row_in.3, s32[2]{0:T(128)} %col_in.3, f32[80,32,128]{2,1,0:T(8,128)} %bitcast.3, f32[2,16,40,128]{3,2,1,0:T(8,128)} %shard_map.91.obs_in, s32[2,1024]{1,0:T(2,128)} %ox_in.3, s32[2,1024]{1,0:T(2,128)} %oy_in.3, s32[2,1024]{1,0:T(2,128)} %ol_in.3, f32[2,1024]{1,0:T(2,128)} %value_in.1, ...), custom_call_target="tpu_custom_call" | custom-call | tf_op jit(solution)/shard_map/pallas_call | solution.py:280

commit v7 on v6

--- a/solution.py
+++ b/solution.py
@@ -59,7 +59,7 @@
 
 
 def update_kernel(row_in, col_in, state, obs_in, ox_in, oy_in, ol_in, value_in, noise_in, var_in, out,
-                  row, col, ox, oy, ol, value, var, obs, noises, cells, hx, both, scaled, cast, weights, near_y, col_x, col_y, col_f, taper, keep, gain_hi, gain_lo,
+                  row, col, ox, oy, ol, value, var, obs, noises, cells, hx, gap, lines, scaled, cast, weights, near_y, col_x, col_y, col_f, taper, keep, gain_hi, gain_lo,
                   sem_in, sem_small, sem_out):
     gx = lax.axis_index("gx")
     gy = lax.axis_index("gy")
@@ -105,15 +105,16 @@
         lane = lax.broadcasted_iota(jnp.int32, (1, 128), 1)
         mesh_y = (gy * 128 + lane - col[b] * 128).astype(F32) * (1.0 / LOC)
 
-        @pl.loop(0, 8, unroll=4)
+        @pl.loop(0, 8, unroll=8)
         def _(c):
             cols = pl.ds(pl.multiple_of(c * 128, 128), 128)
             h = members_of(source, c)
             inv = 1.0 / var[b : b + 1, cols]
             o = h - jnp.sum(h, axis=0, keepdims=True) * (1.0 / MEMBERS)
             d = value[b : b + 1, cols] + noises[b, :, cols] - h
-            both[0:MEMBERS, cols] = o
-            both[MEMBERS : 2 * MEMBERS, cols] = d
+            gap[:, cols] = d
+            hi, lo = split(o)
+            lines[:, cols] = jnp.concatenate([hi, lo, hi, jnp.zeros((16, 128), BF16)], axis=0)
             for n, part in enumerate((o * inv, d * inv)):
                 hi, lo = split(part)
                 scaled[n * MEMBERS : (n + 1) * MEMBERS, cols] = hi
@@ -154,7 +155,9 @@
         inner = inner + jnp.where(eye, MEMBERS - 1.0, 0.0) + trace * (1.0 / MEMBERS / MEMBERS)
         inverse = inverse_of(inner, keep)
         factor = dot(gram[MEMBERS : 2 * MEMBERS], inverse, NN, HIGH)
-        w = both[MEMBERS : 2 * MEMBERS] - dot(factor, both[0:MEMBERS], NN, HIGH)
+        hi = factor.astype(BF16).astype(F32)
+        factor = jnp.concatenate([hi, hi, factor - hi, jnp.zeros((MEMBERS, 16), F32)], axis=1).astype(BF16)
+        w = gap[...] - dot(factor, lines[...])
         w = w * (1.0 / var[b : b + 1, :])
         hi, lo = split(w)
         weights[0:MEMBERS] = hi
@@ -294,7 +297,8 @@
             S((2, MEMBERS, 1024), F32),
             S((32, MEMBERS, 128), F32),
             S((16, 40, 128), F32),
-            S((160, 1024), F32),
+            S((MEMBERS, 1024), F32),
+            S((256, 1024), BF16),
             S((4 * MEMBERS, 1024), BF16),
             S((5, 1024, 256), BF16),
             S((160, 1024), BF16),
@@ -341,8 +345,25 @@
         return (yy * 4 + t // 2, (t % 2) * 8 + xx * 2 + core)
 
     mate = (gx, zl * 8 + xx * 2 + other)
-    ahead = [((yy + dy) % 4) * 4 + (xx + dx) % 4 for dx, dy in FAR]
-    behind = [((yy + 4 - dy) % 4) * 4 + (xx + 4 - dx) % 4 for dx, dy in reversed(FAR)]
+    x_at = [xx] + [(xx + d) % 4 for d in range(1, 4)]
+    y_at = [yy] + [(yy + d) % 4 for d in range(1, 4)]
+    z_at = [z] + [(z + d) % 8 for d in range(1, 8)]
+    ahead = [(x_at[dx], y_at[dy]) for dx, dy in FAR]
+    behind = [(x_at[-dx], y_at[-dy]) for dx, dy in reversed(FAR)]
+
+    def dev(x, y):
+        return (y * 4 + zh, zl * 8 + x * 2 + core)
+
+    barrier = pltpu.get_barrier_semaphore()
+
+    def greet(to):
+        pl.semaphore_signal(barrier, inc=1, device_id=to, device_id_type=MESH)
+
+    for d in (4, 3, 5, 2, 6, 1, 7):
+        greet(dev_z(z_at[d]))
+    for x, y in ahead:
+        greet(dev(x, y))
+    greet(mate)
 
     small = [(row_in, row), (col_in, col), (ox_in, ox), (oy_in, oy), (ol_in, ol)]
     small = [pltpu.make_async_copy(src, dst, sem.at[i]) for i, (src, dst) in enumerate(small)]
@@ -352,18 +373,6 @@
     @pl.loop(0, 32)
     def _(r):
         pltpu.make_async_copy(state.at[:, r], cells.at[r], sem_cells).start()
-
-    barrier = pltpu.get_barrier_semaphore()
-
-    @pl.loop(1, 16)
-    def _(d):
-        pl.semaphore_signal(barrier, inc=1, device_id=dev_xy((q + d) % 16), device_id_type=MESH)
-
-    @pl.loop(1, 8)
-    def _(d):
-        pl.semaphore_signal(barrier, inc=1, device_id=dev_z((z + d) % 8), device_id_type=MESH)
-
-    pl.semaphore_signal(barrier, inc=1, device_id=mate, device_id_type=MESH)
 
     for copy in small:
         copy.wait()
@@ -397,8 +406,8 @@
     def c2(t, slot):
         return remote(z_src, z_buf.at[slot], s2s.at[t], s2r.at[slot], dev_z(t))
 
-    def c3(t, slot):
-        return remote(full.at[slot], full.at[slot], s3s.at[t], s3r.at[slot], dev_xy(t))
+    def c3(x, y, slot):
+        return remote(full.at[slot], full.at[slot], s3s.at[y * 4 + x], s3r.at[slot], dev(x, y))
 
     def c4(b, slot):
         return remote(full.at[slot], out.at[b, slot], s4s.at[slot], s4r.at[slot], mate)
@@ -441,23 +450,25 @@
                 c1(t, q).start()
 
     total = acc[q]
-    for t in behind:
+    for x, y in behind:
+        t = y * 4 + x
         c1(t, t).wait_recv()
         total = total + ring_buf[t]
     z_src[...] = total
     for d in (4, 3, 5, 2, 6, 1, 7):
-        c2((z + d) % 8, z).start()
+        c2(z_at[d], z).start()
     for d in (1, 7, 2, 6, 3, 5, 4):
-        t = (z + 8 - d) % 8
+        t = z_at[-d]
         c2(t, t).wait_recv()
         total = total + z_buf[t]
     full[q] = total
-    for t in ahead:
-        c3(t, q).start()
+    for x, y in ahead:
+        c3(x, y, q).start()
     c4(core, q).start()
     keep(q).start()
-    for t in behind:
-        c3(t, t).wait_recv()
+    for x, y in behind:
+        t = y * 4 + x
+        c3(x, y, t).wait_recv()
         c4(core, t).start()
         keep(t).start()
 
@@ -478,7 +489,7 @@
     def _(d):
         t = (q + d) % 16
         c1(t, q).wait_send()
-        c3(t, q).wait_send()
+        c3(t % 4, t // 4, q).wait_send()
 
     @pl.loop(1, 8)
     def _(d):

time: 61.5 us -> 47.5 us (0.77)
  the two profiles are of different devices: /device:TPU:57 before, /device:TPU:1 now
where the time goes in v7:
time: 47.5 us; the launch traced here: 47.3 us
  Pallas kernels  47.1 us (99%)
    pallas_call x1, Pallas kernels, spread(): pl.pallas_call(spread_kernel, out_shape=jax.ShapeDtypeStruct((2, 16, 40,...  34.5 us
    pallas_call x1, Pallas kernels, update(): pl.pallas_call(update_kernel, out_shape=jax.ShapeDtypeStruct(state.shape,...  12.6 us

profile of v7, /device:TPU:1, one launch (start us, length us, event | category | flops | bytes accessed | tf_op | source)
XLA Modules:
  0.0 47.3 jit_solution(10770164951366418461)
XLA Ops:
  0.0 34.5 %shard_map.91.obs_in = f32[2,16,40,128]{3,2,1,0:T(8,128)} custom-call(s32[2]{0:T(128)} %row_in.3, s32[2]{0:T(128)} %col_in.3, f32[80,32,128]{2,1,0:T(8,128)} %bitcast.2, s32[2,1024]{1,0:T(2,128)} %ox_in.3, s32[2,1024]{1,0:T(2,128)} %oy_in.3, s32[2,1024]{1,0:T(2,128)} %ol_in.3), custom_call_target="tpu_custom_call" | custom-call | tf_op jit(solution)/shard_map/pallas_call | solution.py:502
  34.5 12.6 %shard_map.92 = f32[80,32,128]{2,1,0:T(8,128)} custom-call(s32[2]{0:T(128)} %row_in.3, s32[2]{0:T(128)} %col_in.3, f32[80,32,128]{2,1,0:T(8,128)} %bitcast.3, f32[2,16,40,128]{3,2,1,0:T(8,128)} %shard_map.91.obs_in, s32[2,1024]{1,0:T(2,128)} %ox_in.3, s32[2,1024]{1,0:T(2,128)} %oy_in.3, s32[2,1024]{1,0:T(2,128)} %ol_in.3, f32[2,1024]{1,0:T(2,128)} %value_in.1, ...), custom_call_target="tpu_custom_call" | custom-call | tf_op jit(solution)/shard_map/pallas_call | solution.py:283
